TPU v7x, 256 devices: a whole 4x4x8 slice. The times are simulated.
256 devices in a mesh: gy: 16 (over x_lo, y, core), gz: 16 (over z, x_hi).
Axes of the slice: x: 4 (x_hi: 2, x_lo: 2; x = x_hi * 2 + x_lo), y: 4, z: 8, core: 2. Of those that a mesh axis runs over, the one named last changes fastest.
Arguments:
- phase: int32 [256, 256, 128], P('gy', 'gz'), may hold values from 0 to 1, as said below
- density: float32 [256, 256, 128], P('gy', 'gz'), may hold values from 0.8 to 1.2
- velocity: float32 [3, 256, 256, 128], P(None, 'gy', 'gz'), may hold values from -0.18 to 0.18
Outputs:
- density_red: float32 [256, 256, 128], P('gy', 'gz')
- density_blue: float32 [256, 256, 128], P('gy', 'gz')
- momentum: float32 [3, 256, 256, 128], P(None, 'gy', 'gz')
Inputs may be any that keep to these rules, and one draw needn't show every extreme that they name: `phase`: 1 marks the liquid films of a periodic Weaire-Phelan foam (Voronoi cells of a jittered A15 lattice with cubic period 32); both labels occur.
All inputs are finite; a program needn't handle non-finite values.
Results may differ from a plain program's by a relative error of at most 0.00011.
Values sent between devices are 32-bit elements; how exact they have to be, the bound alone decides.
No kernel may reach another device: no remote copies, remote signals or barrier semaphores. Data moves between devices by JAX's collectives and lax.ppermute only.
A program may use at most 128 MiB of HBM per device.

v0:
```python
import math

import jax
import jax.numpy as jnp
from jax import lax
from jax.sharding import PartitionSpec as P

STEPS = 2


VELOCITIES = [
    [0, 0, 0],
    [1, 0, 0],
    [-1, 0, 0],
    [0, 1, 0],
    [0, -1, 0],
    [0, 0, 1],
    [0, 0, -1],
    [1, 1, 0],
    [-1, -1, 0],
    [1, -1, 0],
    [-1, 1, 0],
    [1, 0, 1],
    [-1, 0, -1],
    [1, 0, -1],
    [-1, 0, 1],
    [0, 1, 1],
    [0, -1, -1],
    [0, 1, -1],
    [0, -1, 1],
]
BOTH_SETS = VELOCITIES + VELOCITIES
LATTICE_WEIGHTS = [1.0 / 3.0] + [1.0 / 18.0] * 6 + [1.0 / 36.0] * 12
BIASES = [-1.0 / 3.0] + [1.0 / 18.0] * 6 + [1.0 / 36.0] * 12
relax_time = 0.8
surface_amp = 0.05
recolouring_strength = 0.7
grad_floor = 0.05


def with_halo(block, sides, width):
    for axis, dim in sides:
        count = lax.axis_size(axis)
        forward = [(i, i + 1) for i in range(count - 1)]
        forward.append((count - 1, 0))
        backward = [(target, source) for source, target in forward]
        low = lax.ppermute(
            lax.slice_in_dim(block, block.shape[dim] - width, None, axis=dim), axis, forward
        )
        high = lax.ppermute(lax.slice_in_dim(block, 0, width, axis=dim), axis, backward)
        block = jnp.concatenate([low, block, high], axis=dim)
    return block


def equilibrium(dens_in, vel_x, vel_y, vel_z):
    speed_sq = vel_x * vel_x + vel_y * vel_y + vel_z * vel_z
    result = []
    for site_index in range(19):
        c_x, c_y, c_z = [float(v) for v in VELOCITIES[site_index]]
        along_direction = c_x * vel_x + c_y * vel_y + c_z * vel_z
        result.append(
            LATTICE_WEIGHTS[site_index]
            * dens_in
            * (
                1.0
                + 3.0 * along_direction
                + 4.5 * along_direction * along_direction
                - 1.5 * speed_sq
            )
        )
    return jnp.stack(result)


def moments(total_pop):
    mom_x = (
        total_pop[1]
        - total_pop[2]
        + total_pop[7]
        - total_pop[8]
        + total_pop[9]
        - total_pop[10]
        + total_pop[11]
        - total_pop[12]
        + total_pop[13]
        - total_pop[14]
    )
    mom_y = (
        total_pop[3]
        - total_pop[4]
        + total_pop[7]
        - total_pop[8]
        - total_pop[9]
        + total_pop[10]
        + total_pop[15]
        - total_pop[16]
        + total_pop[17]
        - total_pop[18]
    )
    mom_z = (
        total_pop[5]
        - total_pop[6]
        + total_pop[11]
        - total_pop[12]
        - total_pop[13]
        + total_pop[14]
        + total_pop[15]
        - total_pop[16]
        - total_pop[17]
        + total_pop[18]
    )
    return (mom_x, mom_y, mom_z)


def densities(red_pop, blue_pop):
    rho_red = jnp.sum(red_pop, axis=0)
    rho_blue = jnp.sum(blue_pop, axis=0)
    dens_all = rho_red + rho_blue
    colour = (rho_red - rho_blue) / dens_all
    return (rho_red, rho_blue, dens_all, colour)


def collide(red_pop, blue_pop, rho_red, rho_blue, dens_all, nearby):
    grad_x = jnp.zeros_like(dens_all)
    grad_y = jnp.zeros_like(dens_all)
    grad_z = jnp.zeros_like(dens_all)
    for site_index in range(1, 19):
        c_x, c_y, c_z = [float(v) for v in VELOCITIES[site_index]]
        scaled = 3.0 * LATTICE_WEIGHTS[site_index] * nearby[site_index]
        grad_x = grad_x + c_x * scaled
        grad_y = grad_y + c_y * scaled
        grad_z = grad_z + c_z * scaled
    gmag = jnp.sqrt(grad_x * grad_x + grad_y * grad_y + grad_z * grad_z)
    gradient_divisor = jnp.maximum(gmag, grad_floor)
    total_pop = red_pop + blue_pop
    mom_x, mom_y, mom_z = moments(total_pop)
    feq = equilibrium(dens_all, mom_x / dens_all, mom_y / dens_all, mom_z / dens_all)
    share = rho_red / dens_all
    mixing_fraction = rho_red * rho_blue / dens_all
    red_out = []
    blue_out = []
    for site_index in range(19):
        c_x, c_y, c_z = [float(v) for v in VELOCITIES[site_index]]
        along_direction = c_x * grad_x + c_y * grad_y + c_z * grad_z
        post = (
            total_pop[site_index]
            - (total_pop[site_index] - feq[site_index]) / relax_time
            + 0.5
            * surface_amp
            * (
                LATTICE_WEIGHTS[site_index] * along_direction * along_direction / gradient_divisor
                - BIASES[site_index] * gmag
            )
        )
        red_updated = share * post
        if site_index > 0:
            domain_length = math.sqrt(c_x * c_x + c_y * c_y + c_z * c_z)
            red_updated = red_updated + recolouring_strength * mixing_fraction * LATTICE_WEIGHTS[
                site_index
            ] * along_direction / (domain_length * gradient_divisor)
        red_out.append(red_updated)
        blue_out.append(post - red_updated)
    return (jnp.stack(red_out), jnp.stack(blue_out))


def finish(red_pop, blue_pop):
    density_red = jnp.sum(red_pop, axis=0)
    density_blue = jnp.sum(blue_pop, axis=0)
    mom_x, mom_y, mom_z = moments(red_pop + blue_pop)
    return (density_red, density_blue, jnp.stack([mom_x, mom_y, mom_z]))


def shards(phase, density, velocity):
    rows_y = phase.shape[0]
    rows_z = phase.shape[1]
    label = phase.astype(jnp.float32)
    red_pop = equilibrium(label * density, velocity[0], velocity[1], velocity[2])
    blue_pop = equilibrium((1.0 - label) * density, velocity[0], velocity[1], velocity[2])
    for step in range(STEPS):
        rho_red, rho_blue, dens_all, colour = densities(red_pop, blue_pop)
        padded = with_halo(colour, (("gy", 0), ("gz", 1)), 1)
        nearby = []
        for site_index in range(19):
            c_x, c_y, c_z = [int(v) for v in VELOCITIES[site_index]]
            window = padded[1 + c_y : 1 + c_y + rows_y, 1 + c_z : 1 + c_z + rows_z]
            nearby.append(jnp.roll(window, -c_x, axis=2))
        red_post, blue_post = collide(red_pop, blue_pop, rho_red, rho_blue, dens_all, nearby)
        stacked = jnp.concatenate([red_post, blue_post], axis=0)
        framed = with_halo(stacked, (("gy", 1), ("gz", 2)), 1)
        moved = []
        for site_index in range(38):
            c_x, c_y, c_z = [int(v) for v in BOTH_SETS[site_index]]
            window = framed[site_index, 1 - c_y : 1 - c_y + rows_y, 1 - c_z : 1 - c_z + rows_z]
            moved.append(jnp.roll(window, c_x, axis=2))
        read = jnp.stack(moved)
        red_pop = read[:19]
        blue_pop = read[19:]
    return finish(red_pop, blue_pop)


def solution(mesh):
    placed = (P("gy", "gz", None), P("gy", "gz", None), P(None, "gy", "gz", None))
    return jax.shard_map(
        shards,
        mesh=mesh,
        in_specs=placed,
        out_specs=(P("gy", "gz", None), P("gy", "gz", None), P(None, "gy", "gz", None)),
        check_vma=False,
    )
```

profile of v0, /device:TPU:102, one launch (start us, length us, event | category | flops | bytes accessed | tf_op | source)
XLA Modules:
  0.0 118.0 jit_solution(6381350524203153372)
XLA Ops:
  0.6 2.2 %subtract_divide_fusion.3 = (f32[16,16,128]{2,1,0:T(8,128)S(1)}, f32[16,16,128]{2,1,0:T(8,128)S(1)}, f32[16,16,128]{2,1,0:T(8,128)S(1)}, f32[16,16,128]{2,1,0:T(...) fusion(f32[16,16,128]{2,1,0:T(8,128)} %param.4, ...), kind=kLoop, calls=%fused_computation.1101 | loop fusion | flops 7897088 | bytes 3932160 | tf_op jit(solution)/shard_map/div | solution.py:118
  2.9 3.8 %collective-permute-start = (f32[1,16,128]{2,1,0:T(8,128)S(1)}, f32[1,16,128]{2,1,0:T(8,128)S(1)}, u32[]{:S(2)}, u32[]{:S(2)}) collective-permute-start(f32[1,16,128]{2,1,0:T(8,128)S(1)} %get-tuple-element.350), channel_id=1, source_target_pairs={{16,0},{32,16},{48,32},{64,48},{80,64},{96,80},{112,96},{128,112},... | collective-permute-start | bytes 24584 | tf_op jit(solution)/shard_map/ppermute | solution.py:50
  8.2 4.0 %collective-permute-start.3 = (f32[18,1,128]{2,1,0:T(1,128)S(1)}, f32[18,1,128]{2,1,0:T(1,128)S(1)}, u32[]{:S(2)}, u32[]{:S(2)}) collective-permute-start(f32[18,1,128]{2,1,0:T(1,128)S(1)} %get-tuple-element.317), channel_id=1, source_target_pairs={{0,1},{1,2},{2,3},{3,4},{4,5},{5,6},{6,7},{7,8},{8,9},{9,10},{10,1... | collective-permute-start | bytes 27656 | tf_op jit(solution)/shard_map/ppermute | solution.py:47
  12.7 0.9 collective-permute-done.3
  13.6 5.9 %collective-permute-done.2 = f32[18,1,128]{2,1,0:T(1,128)S(1)} collective-permute-done((f32[18,1,128]{2,1,0:T(1,128)S(1)}, f32[18,1,128]{2,1,0:T(1,128)S(1)}, u32[]{:S(2)}, u32[]{:S(2)}) %collective-permute-start.2) | collective-permute-done | bytes 9248 | tf_op jit(solution)/shard_map/ppermute | solution.py:50
  19.8 1.0 constant_dynamic-update-slice_fusion.113
  24.4 3.8 %collective-permute-start.5 = (f32[38,1,16,128]{3,2,1,0:T(8,128)S(1)}, f32[38,1,16,128]{3,2,1,0:T(8,128)S(1)}, u32[]{:S(2)}, u32[]{:S(2)}) collective-permute-start(f32[38,1,16,128]{3,2,1,0:T(8,128)S(1)} %get-tuple-element.290), channel_id=1, source_target_pairs={{16,0},{32,16},{48,32},{64,48},{80,64},{96,80},{112,96},{128,112},... | collective-permute-start | bytes 933896 | tf_op jit(solution)/shard_map/ppermute | solution.py:50
  28.8 7.7 %collective-permute-done.4 = f32[38,1,16,128]{3,2,1,0:T(8,128)S(1)} collective-permute-done((f32[38,1,16,128]{3,2,1,0:T(8,128)S(1)}, f32[38,1,16,128]{3,2,1,0:T(8,128)S(1)}, u32[]{:S(2)}, u32[]{:S(2)}) %collective-permute-start.4) | collective-permute-done | bytes 311328 | tf_op jit(solution)/shard_map/ppermute | solution.py:47
  36.5 5.2 %collective-permute-done.5 = f32[38,1,16,128]{3,2,1,0:T(8,128)S(1)} collective-permute-done((f32[38,1,16,128]{3,2,1,0:T(8,128)S(1)}, f32[38,1,16,128]{3,2,1,0:T(8,128)S(1)}, u32[]{:S(2)}, u32[]{:S(2)}) %collective-permute-start.5) | collective-permute-done | bytes 311328 | tf_op jit(solution)/shard_map/ppermute | solution.py:50
  41.8 0.5 pad_maximum_fusion.4
  42.5 3.6 %collective-permute-start.7 = (f32[38,18,1,128]{3,2,1,0:T(1,128)S(1)}, f32[38,18,1,128]{3,2,1,0:T(1,128)S(1)}, u32[]{:S(2)}, u32[]{:S(2)}) collective-permute-start(f32[38,18,1,128]{3,2,1,0:T(1,128)S(1)} %get-tuple-element.260), channel_id=1, source_target_pairs={{1,0},{2,1},{3,2},{4,3},{5,4},{6,5},{7,6},{8,7},{9,8},{10,9},{11,1... | collective-permute-start | bytes 1050632 | tf_op jit(solution)/shard_map/ppermute | solution.py:50
  46.8 8.1 %collective-permute-done.6 = f32[38,18,1,128]{3,2,1,0:T(1,128)S(1)} collective-permute-done((f32[38,18,1,128]{3,2,1,0:T(1,128)S(1)}, f32[38,18,1,128]{3,2,1,0:T(1,128)S(1)}, u32[]{:S(2)}, u32[]{:S(2)}) %collective-permute-start.6) | collective-permute-done | bytes 350240 | tf_op jit(solution)/shard_map/ppermute | solution.py:47
  56.1 1.3 %subtract_divide_fusion = (f32[16,16,128]{2,1,0:T(8,128)S(1)}, f32[16,16,128]{2,1,0:T(8,128)S(1)}, f32[16,16,128]{2,1,0:T(8,128)S(1)}, f32[1,16,16,128]{3,2,1,0:...) fusion(f32[16,16,1]{2,1,0:T(8,128)S(1)} %bitcast.1258, ...), kind=kLoop, calls=%fused_computation.1069 | loop fusion | flops 3309568 | bytes 11808768 | tf_op jit(solution)/shard_map/div | solution.py:118
  59.4 3.8 %collective-permute-start.8 = (f32[1,16,128]{2,1,0:T(8,128)S(1)}, f32[1,16,128]{2,1,0:T(8,128)S(1)}, u32[]{:S(2)}, u32[]{:S(2)}) collective-permute-start(f32[1,16,128]{2,1,0:T(8,128)S(1)} %get-tuple-element.338), channel_id=1, source_target_pairs={{16,0},{32,16},{48,32},{64,48},{80,64},{96,80},{112,96},{128,112},... | collective-permute-start | bytes 24584 | tf_op jit(solution)/shard_map/ppermute | solution.py:50
  63.4 0.4 add.1847
  63.8 0.8 collective-permute-done.9
  64.7 3.5 %collective-permute-start.10 = (f32[18,1,128]{2,1,0:T(1,128)S(1)}, f32[18,1,128]{2,1,0:T(1,128)S(1)}, u32[]{:S(2)}, u32[]{:S(2)}) collective-permute-start(f32[18,1,128]{2,1,0:T(1,128)S(1)} %get-tuple-element.314), channel_id=1, source_target_pairs={{1,0},{2,1},{3,2},{4,3},{5,4},{6,5},{7,6},{8,7},{9,8},{10,9},{11,1... | collective-permute-start | bytes 27656 | tf_op jit(solution)/shard_map/ppermute | solution.py:50
  68.7 1.2 collective-permute-done.11
  69.8 2.4 %collective-permute-done.10 = f32[18,1,128]{2,1,0:T(1,128)S(1)} collective-permute-done((f32[18,1,128]{2,1,0:T(1,128)S(1)}, f32[18,1,128]{2,1,0:T(1,128)S(1)}, u32[]{:S(2)}, u32[]{:S(2)}) %collective-permute-start.10) | collective-permute-done | bytes 9248 | tf_op jit(solution)/shard_map/ppermute | solution.py:50
  72.7 1.0 constant_dynamic-update-slice_fusion.189
  77.5 2.8 %collective-permute-start.13 = (f32[38,1,16,128]{3,2,1,0:T(8,128)S(1)}, f32[38,1,16,128]{3,2,1,0:T(8,128)S(1)}, u32[]{:S(2)}, u32[]{:S(2)}) collective-permute-start(f32[38,1,16,128]{3,2,1,0:T(8,128)S(1)} %get-tuple-element.284), channel_id=1, source_target_pairs={{16,0},{32,16},{48,32},{64,48},{80,64},{96,80},{112,96},{128,112},... | collective-permute-start | bytes 933896 | tf_op jit(solution)/shard_map/ppermute | solution.py:50
  80.7 4.1 %collective-permute-done.13 = f32[38,1,16,128]{3,2,1,0:T(8,128)S(1)} collective-permute-done((f32[38,1,16,128]{3,2,1,0:T(8,128)S(1)}, f32[38,1,16,128]{3,2,1,0:T(8,128)S(1)}, u32[]{:S(2)}, u32[]{:S(2)}) %collective-permute-start.13) | collective-permute-done | bytes 311328 | tf_op jit(solution)/shard_map/ppermute | solution.py:50
  84.8 8.5 %collective-permute-done.12 = f32[38,1,16,128]{3,2,1,0:T(8,128)S(1)} collective-permute-done((f32[38,1,16,128]{3,2,1,0:T(8,128)S(1)}, f32[38,1,16,128]{3,2,1,0:T(8,128)S(1)}, u32[]{:S(2)}, u32[]{:S(2)}) %collective-permute-start.12) | collective-permute-done | bytes 311328 | tf_op jit(solution)/shard_map/ppermute | solution.py:47
  93.3 0.5 pad_maximum_fusion.1
  93.8 6.5 %collective-permute-start.14 = (f32[38,18,1,128]{3,2,1,0:T(1,128)S(1)}, f32[38,18,1,128]{3,2,1,0:T(1,128)S(1)}, u32[]{:S(2)}, u32[]{:S(2)}) collective-permute-start(f32[38,18,1,128]{3,2,1,0:T(1,128)S(1)} %get-tuple-element.259), channel_id=1, source_target_pairs={{0,1},{1,2},{2,3},{3,4},{4,5},{5,6},{6,7},{7,8},{8,9},{9,10},{10,1... | collective-permute-start | bytes 1050632 | tf_op jit(solution)/shard_map/ppermute | solution.py:47
  100.4 0.3 collective-permute-start.15
  101.5 3.7 %collective-permute-done.14 = f32[38,18,1,128]{3,2,1,0:T(1,128)S(1)} collective-permute-done((f32[38,18,1,128]{3,2,1,0:T(1,128)S(1)}, f32[38,18,1,128]{3,2,1,0:T(1,128)S(1)}, u32[]{:S(2)}, u32[]{:S(2)}) %collective-permute-start.14) | collective-permute-done | bytes 350240 | tf_op jit(solution)/shard_map/ppermute | solution.py:47
  105.7 6.0 %collective-permute-done.15 = f32[38,18,1,128]{3,2,1,0:T(1,128)S(1)} collective-permute-done((f32[38,18,1,128]{3,2,1,0:T(1,128)S(1)}, f32[38,18,1,128]{3,2,1,0:T(1,128)S(1)}, u32[]{:S(2)}, u32[]{:S(2)}) %collective-permute-start.15) | collective-permute-done | bytes 350240 | tf_op jit(solution)/shard_map/ppermute | solution.py:50
  114.4 0.4 add.2045
  115.1 0.8 pad_maximum_fusion
  115.8 1.1 bitcast_add_fusion.8
  116.9 1.1 bitcast_add_fusion
  (239 shorter events, 19.0 us)
Async XLA Ops:
  2.9 5.3 %collective-permute-start.1 = (f32[1,16,128]{2,1,0:T(8,128)S(1)}, f32[1,16,128]{2,1,0:T(8,128)S(1)}, u32[]{:S(2)}, u32[]{:S(2)}) collective-permute-start(f32[1,16,128]{2,1,0:T(8,128)S(1)} %get-tuple-element.349), channel_id=1, source_target_pairs={{0,16},{16,32},{32,48},{48,64},{64,80},{80,96},{96,112},{112,128},... | collective-permute-start | bytes 24584 | tf_op jit(solution)/shard_map/ppermute | solution.py:47
  2.9 5.2 %collective-permute-start = (f32[1,16,128]{2,1,0:T(8,128)S(1)}, f32[1,16,128]{2,1,0:T(8,128)S(1)}, u32[]{:S(2)}, u32[]{:S(2)}) collective-permute-start(f32[1,16,128]{2,1,0:T(8,128)S(1)} %get-tuple-element.350), channel_id=1, source_target_pairs={{16,0},{32,16},{48,32},{64,48},{80,64},{96,80},{112,96},{128,112},... | collective-permute-start | bytes 24584 | tf_op jit(solution)/shard_map/ppermute | solution.py:50
  8.2 5.4 %collective-permute-start.3 = (f32[18,1,128]{2,1,0:T(1,128)S(1)}, f32[18,1,128]{2,1,0:T(1,128)S(1)}, u32[]{:S(2)}, u32[]{:S(2)}) collective-permute-start(f32[18,1,128]{2,1,0:T(1,128)S(1)} %get-tuple-element.317), channel_id=1, source_target_pairs={{0,1},{1,2},{2,3},{3,4},{4,5},{5,6},{6,7},{7,8},{8,9},{9,10},{10,1... | collective-permute-start | bytes 27656 | tf_op jit(solution)/shard_map/ppermute | solution.py:47
  12.2 7.3 %collective-permute-start.2 = (f32[18,1,128]{2,1,0:T(1,128)S(1)}, f32[18,1,128]{2,1,0:T(1,128)S(1)}, u32[]{:S(2)}, u32[]{:S(2)}) collective-permute-start(f32[18,1,128]{2,1,0:T(1,128)S(1)} %get-tuple-element.318), channel_id=1, source_target_pairs={{1,0},{2,1},{3,2},{4,3},{5,4},{6,5},{7,6},{8,7},{9,8},{10,9},{11,1... | collective-permute-start | bytes 27656 | tf_op jit(solution)/shard_map/ppermute | solution.py:50
  24.3 12.3 %collective-permute-start.4 = (f32[38,1,16,128]{3,2,1,0:T(8,128)S(1)}, f32[38,1,16,128]{3,2,1,0:T(8,128)S(1)}, u32[]{:S(2)}, u32[]{:S(2)}) collective-permute-start(f32[38,1,16,128]{3,2,1,0:T(8,128)S(1)} %get-tuple-element.289), channel_id=1, source_target_pairs={{0,16},{16,32},{32,48},{48,64},{64,80},{80,96},{96,112},{112,128},... | collective-permute-start | bytes 933896 | tf_op jit(solution)/shard_map/ppermute | solution.py:47
  24.4 17.4 %collective-permute-start.5 = (f32[38,1,16,128]{3,2,1,0:T(8,128)S(1)}, f32[38,1,16,128]{3,2,1,0:T(8,128)S(1)}, u32[]{:S(2)}, u32[]{:S(2)}) collective-permute-start(f32[38,1,16,128]{3,2,1,0:T(8,128)S(1)} %get-tuple-element.290), channel_id=1, source_target_pairs={{16,0},{32,16},{48,32},{64,48},{80,64},{96,80},{112,96},{128,112},... | collective-permute-start | bytes 933896 | tf_op jit(solution)/shard_map/ppermute | solution.py:50
  42.3 12.6 %collective-permute-start.6 = (f32[38,18,1,128]{3,2,1,0:T(1,128)S(1)}, f32[38,18,1,128]{3,2,1,0:T(1,128)S(1)}, u32[]{:S(2)}, u32[]{:S(2)}) collective-permute-start(f32[38,18,1,128]{3,2,1,0:T(1,128)S(1)} %get-tuple-element.261), channel_id=1, source_target_pairs={{0,1},{1,2},{2,3},{3,4},{4,5},{5,6},{6,7},{7,8},{8,9},{9,10},{10,1... | collective-permute-start | bytes 1050632 | tf_op jit(solution)/shard_map/ppermute | solution.py:47
  42.5 13.0 %collective-permute-start.7 = (f32[38,18,1,128]{3,2,1,0:T(1,128)S(1)}, f32[38,18,1,128]{3,2,1,0:T(1,128)S(1)}, u32[]{:S(2)}, u32[]{:S(2)}) collective-permute-start(f32[38,18,1,128]{3,2,1,0:T(1,128)S(1)} %get-tuple-element.260), channel_id=1, source_target_pairs={{1,0},{2,1},{3,2},{4,3},{5,4},{6,5},{7,6},{8,7},{9,8},{10,9},{11,1... | collective-permute-start | bytes 1050632 | tf_op jit(solution)/shard_map/ppermute | solution.py:50
  59.3 5.3 %collective-permute-start.9 = (f32[1,16,128]{2,1,0:T(8,128)S(1)}, f32[1,16,128]{2,1,0:T(8,128)S(1)}, u32[]{:S(2)}, u32[]{:S(2)}) collective-permute-start(f32[1,16,128]{2,1,0:T(8,128)S(1)} %get-tuple-element.337), channel_id=1, source_target_pairs={{0,16},{16,32},{32,48},{48,64},{64,80},{80,96},{96,112},{112,128},... | collective-permute-start | bytes 24584 | tf_op jit(solution)/shard_map/ppermute | solution.py:47
  59.4 5.2 %collective-permute-start.8 = (f32[1,16,128]{2,1,0:T(8,128)S(1)}, f32[1,16,128]{2,1,0:T(8,128)S(1)}, u32[]{:S(2)}, u32[]{:S(2)}) collective-permute-start(f32[1,16,128]{2,1,0:T(8,128)S(1)} %get-tuple-element.338), channel_id=1, source_target_pairs={{16,0},{32,16},{48,32},{64,48},{80,64},{96,80},{112,96},{128,112},... | collective-permute-start | bytes 24584 | tf_op jit(solution)/shard_map/ppermute | solution.py:50
  64.6 5.2 %collective-permute-start.11 = (f32[18,1,128]{2,1,0:T(1,128)S(1)}, f32[18,1,128]{2,1,0:T(1,128)S(1)}, u32[]{:S(2)}, u32[]{:S(2)}) collective-permute-start(f32[18,1,128]{2,1,0:T(1,128)S(1)} %get-tuple-element.313), channel_id=1, source_target_pairs={{0,1},{1,2},{2,3},{3,4},{4,5},{5,6},{6,7},{7,8},{8,9},{9,10},{10,1... | collective-permute-start | bytes 27656 | tf_op jit(solution)/shard_map/ppermute | solution.py:47
  64.7 7.6 %collective-permute-start.10 = (f32[18,1,128]{2,1,0:T(1,128)S(1)}, f32[18,1,128]{2,1,0:T(1,128)S(1)}, u32[]{:S(2)}, u32[]{:S(2)}) collective-permute-start(f32[18,1,128]{2,1,0:T(1,128)S(1)} %get-tuple-element.314), channel_id=1, source_target_pairs={{1,0},{2,1},{3,2},{4,3},{5,4},{6,5},{7,6},{8,7},{9,8},{10,9},{11,1... | collective-permute-start | bytes 27656 | tf_op jit(solution)/shard_map/ppermute | solution.py:50
  77.5 7.2 %collective-permute-start.13 = (f32[38,1,16,128]{3,2,1,0:T(8,128)S(1)}, f32[38,1,16,128]{3,2,1,0:T(8,128)S(1)}, u32[]{:S(2)}, u32[]{:S(2)}) collective-permute-start(f32[38,1,16,128]{3,2,1,0:T(8,128)S(1)} %get-tuple-element.284), channel_id=1, source_target_pairs={{16,0},{32,16},{48,32},{64,48},{80,64},{96,80},{112,96},{128,112},... | collective-permute-start | bytes 933896 | tf_op jit(solution)/shard_map/ppermute | solution.py:50
  80.3 13.0 %collective-permute-start.12 = (f32[38,1,16,128]{3,2,1,0:T(8,128)S(1)}, f32[38,1,16,128]{3,2,1,0:T(8,128)S(1)}, u32[]{:S(2)}, u32[]{:S(2)}) collective-permute-start(f32[38,1,16,128]{3,2,1,0:T(8,128)S(1)} %get-tuple-element.285), channel_id=1, source_target_pairs={{0,16},{16,32},{32,48},{48,64},{64,80},{80,96},{96,112},{112,128},... | collective-permute-start | bytes 933896 | tf_op jit(solution)/shard_map/ppermute | solution.py:47
  93.8 11.4 %collective-permute-start.14 = (f32[38,18,1,128]{3,2,1,0:T(1,128)S(1)}, f32[38,18,1,128]{3,2,1,0:T(1,128)S(1)}, u32[]{:S(2)}, u32[]{:S(2)}) collective-permute-start(f32[38,18,1,128]{3,2,1,0:T(1,128)S(1)} %get-tuple-element.259), channel_id=1, source_target_pairs={{0,1},{1,2},{2,3},{3,4},{4,5},{5,6},{6,7},{7,8},{8,9},{9,10},{10,1... | collective-permute-start | bytes 1050632 | tf_op jit(solution)/shard_map/ppermute | solution.py:47
  100.4 11.3 %collective-permute-start.15 = (f32[38,18,1,128]{3,2,1,0:T(1,128)S(1)}, f32[38,18,1,128]{3,2,1,0:T(1,128)S(1)}, u32[]{:S(2)}, u32[]{:S(2)}) collective-permute-start(f32[38,18,1,128]{3,2,1,0:T(1,128)S(1)} %get-tuple-element.258), channel_id=1, source_target_pairs={{1,0},{2,1},{3,2},{4,3},{5,4},{6,5},{7,6},{8,7},{9,8},{10,9},{11,1... | collective-permute-start | bytes 1050632 | tf_op jit(solution)/shard_map/ppermute | solution.py:50
where the time goes:
time: 118 us
  waiting for transfers between devices  54.8 us (46%)
  starting transfers between devices  32.8 us (28%)
  other arithmetic  23.6 us (20%)
  local copies, waits for them, and re-layouts  4.71 us (4%)
  between operations  2.19 us (2%)
    ppermute x8, waiting for transfers between devices, with_halo(): lax.ppermute(lax.slice_in_dim(block, block.shape[dim] - width, None, axis...  31 us
    ppermute x8, waiting for transfers between devices, with_halo(): lax.ppermute(lax.slice_in_dim(block, 0, width, axis=dim), axis, backward)  23.7 us
    ppermute x8, starting transfers between devices, with_halo(): lax.ppermute(lax.slice_in_dim(block, 0, width, axis=dim), axis, backward)  21.8 us
    unnamed x140, other arithmetic  13.2 us
    ppermute x8, starting transfers between devices, with_halo(): lax.ppermute(lax.slice_in_dim(block, block.shape[dim] - width, None, axis...  11 us
    slice x40, local copies, waits for them, and re-layouts, shards(): moved.append(jnp.roll(window, c_x, axis=2))  3.76 us
    div x2, other arithmetic, densities(): colour = (rho_red - rho_blue) / dens_all  3.49 us
  transfers between devices with their start and end apart: 16, of which 13 were waited for; matrix products, arithmetic and copies ran while one was open for 5% of the time, Pallas kernels for 0%

commit v1 on v0

v1 whole, which is shorter than its diff:
```python
import math

import jax
import jax.numpy as jnp
from jax import lax
from jax.experimental import pallas as pl
from jax.experimental.pallas import tpu as pltpu
from jax.sharding import PartitionSpec as P

VELOCITIES = [
    [0, 0, 0],
    [1, 0, 0],
    [-1, 0, 0],
    [0, 1, 0],
    [0, -1, 0],
    [0, 0, 1],
    [0, 0, -1],
    [1, 1, 0],
    [-1, -1, 0],
    [1, -1, 0],
    [-1, 1, 0],
    [1, 0, 1],
    [-1, 0, -1],
    [1, 0, -1],
    [-1, 0, 1],
    [0, 1, 1],
    [0, -1, -1],
    [0, 1, -1],
    [0, -1, 1],
]
INDEX = {tuple(v): i for i, v in enumerate(VELOCITIES)}
relax_time = 0.8
surface_amp = 0.05
recolouring_strength = 0.7
grad_floor = 0.05

WIDE = 4
VMEM = pltpu.CompilerParams(vmem_limit_bytes=48 * 1024 * 1024)


def rolled(value, shift):
    return pltpu.roll(value, shift % 128, 1) if shift else value


def fill_z(msg, low, phase, density, velocity):
    thin, wide = (0, 0) if low else (16 - 3, 16 - 4)
    msg[:, 0:3, :] = density[:, thin : thin + 3, :]
    for axis in range(3):
        msg[:, 3 + 3 * axis : 6 + 3 * axis, :] = velocity[axis, :, thin : thin + 3, :]
    msg[:, 12:16, :] = phase[:, wide : wide + 4, :].astype(jnp.float32)


def pack_z(phase, density, velocity, msg_ev, msg_od):
    odd = lax.rem(lax.axis_index("gz"), 2) == 1

    @pl.when(odd)
    def _():
        fill_z(msg_ev, True, phase, density, velocity)
        fill_z(msg_od, False, phase, density, velocity)

    @pl.when(jnp.logical_not(odd))
    def _():
        fill_z(msg_ev, False, phase, density, velocity)
        fill_z(msg_od, True, phase, density, velocity)


def put_z_halo(ref, row, at, msg, src, high):
    if at == 4:
        start = 20 if high else 0
        ref[row, start : start + 4, :] = msg[src, 12:16, :]
    else:
        start = 20 if high else 1
        ref[row, start : start + 3, :] = msg[src, 3 * at : 3 * at + 3, :]


def own_plane(at, y, phase, density, velocity):
    if at == 0:
        return density[y]
    if at == 4:
        return phase[y].astype(jnp.float32)
    return velocity[at - 1, y]


def fill_y(msg, low, odd_z, phase, density, velocity, from_ev, from_od):
    for at in range(5):
        count = 4 if at == 4 else 3
        for k in range(count):
            y = k if low else 16 - count + k
            row = 3 * at + k
            if at != 4:
                msg[row] = jnp.zeros((24, 128), jnp.float32)
            msg[row, 4:20, :] = own_plane(at, y, phase, density, velocity)

            @pl.when(odd_z)
            def _():
                put_z_halo(msg, row, at, from_ev, y, False)
                put_z_halo(msg, row, at, from_od, y, True)

            @pl.when(jnp.logical_not(odd_z))
            def _():
                put_z_halo(msg, row, at, from_od, y, False)
                put_z_halo(msg, row, at, from_ev, y, True)


def pack_y(phase, density, velocity, from_ev, from_od, msg_ev, msg_od):
    odd_z = lax.rem(lax.axis_index("gz"), 2) == 1
    odd_y = lax.rem(lax.axis_index("gy"), 2) == 1
    args = (odd_z, phase, density, velocity, from_ev, from_od)

    @pl.when(odd_y)
    def _():
        fill_y(msg_ev, True, *args)
        fill_y(msg_od, False, *args)

    @pl.when(jnp.logical_not(odd_y))
    def _():
        fill_y(msg_ev, False, *args)
        fill_y(msg_od, True, *args)


def gradient(load):
    near, far = 3.0 / 18.0, 3.0 / 36.0
    mid = load(0, 0)
    up_y, down_y, up_z, down_z = load(1, 0), load(-1, 0), load(0, 1), load(0, -1)
    pp, pm, mp, mm = load(1, 1), load(1, -1), load(-1, 1), load(-1, -1)
    along_x = near * mid + far * ((up_y + down_y) + (up_z + down_z))
    diff_y = up_y - down_y
    diff_z = up_z - down_z
    cross = pp - mm
    other = pm - mp
    grad_x = rolled(along_x, -1) - rolled(along_x, 1)
    grad_y = near * diff_y + far * ((cross + other) + (rolled(diff_y, 1) + rolled(diff_y, -1)))
    grad_z = near * diff_z + far * ((cross - other) + (rolled(diff_z, 1) + rolled(diff_z, -1)))
    return grad_x, grad_y, grad_z


def collide(level, rest_level, tensor, flow, grad, h, share, tail, store_post, store_red):
    def emit(c, post, odd):
        i = INDEX[c]
        if tail is not None:
            post = post + tail[i]
        red = share * post
        if odd is not None:
            red = red + odd
        store_post(i, post)
        store_red(i, red)

    emit((0, 0, 0), rest_level, None)
    xx, yy, zz, xy, xz, yz = tensor
    diag = (xx, yy, zz)
    lev = [level + d for d in diag]
    step = [h * g for g in grad]
    for axis in range(3):
        even = lev[axis] + lev[axis]
        odd = flow[axis] + flow[axis]
        recolour = step[axis] + step[axis]
        c = [0, 0, 0]
        c[axis] = 1
        emit(tuple(c), even + odd, recolour)
        c[axis] = -1
        emit(tuple(c), even - odd, -recolour)
    slant = [s * (1.0 / math.sqrt(2.0)) for s in step]
    for a, b, cross in ((0, 1, xy), (0, 2, xz), (1, 2, yz)):
        base = lev[a] + diag[b]
        twice = cross + cross
        for sign in (1, -1):
            even = base + twice if sign > 0 else base - twice
            odd = flow[a] + flow[b] if sign > 0 else flow[a] - flow[b]
            recolour = slant[a] + slant[b] if sign > 0 else slant[a] - slant[b]
            c = [0, 0, 0]
            c[a], c[b] = 1, sign
            emit(tuple(c), even + odd, recolour)
            emit(tuple(-v for v in c), even - odd, -recolour)


def surface(grad):
    square = grad[0] * grad[0] + grad[1] * grad[1] + grad[2] * grad[2]
    root = lax.rsqrt(jnp.maximum(square, 1e-30))
    return square * root, jnp.minimum(root, 1.0 / grad_floor)


W2 = 1.0 / 36.0


def products(vec, other):
    x, y, z = vec
    p, q, r = other
    return [x * p, y * q, z * r, x * q, x * r, y * r]


def step_one(label, dens, vel, grad, store_post, store_red):
    rho_red = label * dens
    rho_blue = (1.0 - label) * dens
    mix = rho_red * rho_blue / dens
    gmag, inv = surface(grad)
    speed = vel[0] * vel[0] + vel[1] * vel[1] + vel[2] * vel[2]
    scaled = W2 * dens

    def relax(pop, eq):
        return pop - (pop - eq) * (1.0 / relax_time)

    rest = scaled - 1.5 * scaled * speed
    rest = relax(rest, rest)
    flow = [3.0 * scaled * v for v in vel]
    flow = [relax(v, v) for v in flow]
    wide = [(1.5 * f) for f in flow]
    tensor = products(wide, vel)
    pull = (0.5 * surface_amp * W2) * inv
    tensor = [t + s for t, s in zip(tensor, products([pull * g for g in grad], grad))]
    gm = (0.5 * surface_amp * W2) * gmag
    collide(rest - gm, 12.0 * (rest + gm), tensor, flow, grad, (recolouring_strength * W2) * mix * inv, label, None, store_post, store_red)


def step_two(rho, rho_red, pops, grad, store_post, store_red):
    rinv = 1.0 / rho
    share = rho_red * rinv
    mix = share * (rho - rho_red)
    gmag, inv = surface(grad)

    def mom(a):
        total = None
        for i, c in enumerate(VELOCITIES):
            if c[a]:
                term = pops[i]
                total = (term if c[a] > 0 else -term) if total is None else (total + term if c[a] > 0 else total - term)
        return total

    gain = 1.0 / relax_time
    moment = [mom(a) for a in range(3)]
    vel = [m * rinv for m in moment]
    flow = [(3.0 * gain * W2) * m for m in moment]
    half = [1.5 * f for f in flow]
    tensor = products(half, vel)
    rest = (gain * W2) * rho - (1.0 / 3.0) * (tensor[0] + tensor[1] + tensor[2])
    pull = (0.5 * surface_amp * W2) * inv
    tensor = [t + s for t, s in zip(tensor, products([pull * g for g in grad], grad))]
    gm = (0.5 * surface_amp * W2) * gmag
    tail = [(1.0 - gain) * p for p in pops]
    collide(rest - gm, 12.0 * (rest + gm), tensor, flow, grad, (recolouring_strength * W2) * mix * inv, share, tail, store_post, store_red)


def streamed_sum(load, weight=None):
    parts = {0: None, 1: None, -1: None}
    for i, c in enumerate(VELOCITIES):
        w = 1 if weight is None else c[weight]
        if not w:
            continue
        term = load(i)
        held = parts[c[0]]
        parts[c[0]] = (term if w > 0 else -term) if held is None else (held + term if w > 0 else held - term)
    return parts


def compute(phase, density, velocity, z_ev, z_od, y_ev, y_od, out_red, out_blue, out_mom, sign, raw, post1, red1, rho_s, red_s, col_s, post2, red2):
    odd_z = lax.rem(lax.axis_index("gz"), 2) == 1
    odd_y = lax.rem(lax.axis_index("gy"), 2) == 1

    def assemble(row, y):
        for at in range(5):
            ref = sign if at == 4 else raw.at[at]
            ref[row, 4:20, :] = own_plane(at, y, phase, density, velocity)

            @pl.when(odd_z)
            def _():
                put_z_halo(ref, row, at, z_ev, y, False)
                put_z_halo(ref, row, at, z_od, y, True)

            @pl.when(jnp.logical_not(odd_z))
            def _():
                put_z_halo(ref, row, at, z_od, y, False)
                put_z_halo(ref, row, at, z_ev, y, True)

    def assemble_body(y, carry):
        assemble(y + 4, y)
        return carry

    lax.fori_loop(0, 16, assemble_body, 0)

    def take(low, high):
        for at in range(5):
            ref = sign if at == 4 else raw.at[at]
            count = 4 if at == 4 else 3
            for k in range(count):
                ref[4 - count + k, 0:24, :] = low[3 * at + k]
                ref[20 + k, 0:24, :] = high[3 * at + k]

    @pl.when(odd_y)
    def _():
        take(y_ev, y_od)

    @pl.when(jnp.logical_not(odd_y))
    def _():
        take(y_od, y_ev)

    def pass_a(j, carry):
        for k in (0, 8, 16):
            lab = lambda dy, dz: 2.0 * sign[j + 1 + dy, 1 + dz + k : 9 + dz + k, :] - 1.0
            grad = gradient(lab)
            tile = lambda at: raw[at, j + 1, 1 + k : 9 + k, :]

            def store_post(i, v):
                post1[i, j, k : k + 8, :] = v

            def store_red(i, v):
                red1[i, j, k : k + 8, :] = v

            step_one(sign[j + 1, 1 + k : 9 + k, :], tile(0), [tile(1), tile(2), tile(3)], grad, store_post, store_red)
        return carry

    lax.fori_loop(0, 22, pass_a, 0)

    def pass_b(j, carry):
        for k in (0, 8, 16):

            def total(ref):
                def load(i):
                    _, cy, cz = VELOCITIES[i]
                    return ref[i, j + 1 - cy, 1 - cz + k : 9 - cz + k, :]

                parts = streamed_sum(load)
                return parts[0] + (rolled(parts[1], 1) + rolled(parts[-1], -1))

            rho = total(post1)
            red = total(red1)
            rho_s[j, k : k + 8, :] = rho
            red_s[j, k : k + 8, :] = red
            col_s[j, k : k + 8, :] = (red - (rho - red)) / rho
        return carry

    lax.fori_loop(0, 20, pass_b, 0)

    def pass_c(j, carry):
        for k in (0, 8, 16):
            pops = []
            for i, (cx, cy, cz) in enumerate(VELOCITIES):
                pops.append(rolled(post1[i, j + 2 - cy, 2 - cz + k : 10 - cz + k, :], cx))
            grad = gradient(lambda dy, dz: col_s[j + 1 + dy, 1 + dz + k : 9 + dz + k, :])

            def store_post(i, v):
                post2[i, j, k : k + 8, :] = v

            def store_red(i, v):
                red2[i, j, k : k + 8, :] = v

            step_two(rho_s[j + 1, 1 + k : 9 + k, :], red_s[j + 1, 1 + k : 9 + k, :], pops, grad, store_post, store_red)
        return carry

    lax.fori_loop(0, 18, pass_c, 0)

    def pass_d(j, carry):
        for k in (0, 8):

            def load_of(ref):
                def load(i):
                    _, cy, cz = VELOCITIES[i]
                    return ref[i, j + 1 - cy, 1 - cz + k : 9 - cz + k, :]

                return load

            pops = {}

            def load(i):
                if i not in pops:
                    pops[i] = load_of(post2)(i)
                return pops[i]

            def joined(parts):
                side = rolled(parts[1], 1) + rolled(parts[-1], -1)
                return side if parts[0] is None else parts[0] + side

            parts = streamed_sum(load)
            up, down = rolled(parts[1], 1), rolled(parts[-1], -1)
            rho = parts[0] + (up + down)
            red = joined(streamed_sum(load_of(red2)))
            out_red[j, k : k + 8, :] = red
            out_blue[j, k : k + 8, :] = rho - red
            out_mom[0, j, k : k + 8, :] = up - down
            out_mom[1, j, k : k + 8, :] = joined(streamed_sum(load, 1))
            out_mom[2, j, k : k + 8, :] = joined(streamed_sum(load, 2))
        return carry

    lax.fori_loop(0, 16, pass_d, 0)


def f32(*shape):
    return jax.ShapeDtypeStruct(shape, jnp.float32)


def swap(value, axis, first):
    count = lax.axis_size(axis)
    pairs = []
    for low in range(first, count, 2):
        high = (low + 1) % count
        pairs += [(low, high), (high, low)]
    return lax.ppermute(value, axis, pairs)


def shards(phase, density, velocity):
    msg_ev, msg_od = pl.pallas_call(pack_z, out_shape=(f32(16, 16, 128),) * 2, compiler_params=VMEM)(phase, density, velocity)
    z_od = swap(msg_od, "gz", 1)
    z_ev = swap(msg_ev, "gz", 0)
    msg_ev, msg_od = pl.pallas_call(pack_y, out_shape=(f32(16, 24, 128),) * 2, compiler_params=VMEM)(phase, density, velocity, z_ev, z_od)
    y_od = swap(msg_od, "gy", 1)
    y_ev = swap(msg_ev, "gy", 0)
    scratch = [
        pltpu.VMEM((24, 32, 128), jnp.float32),
        pltpu.VMEM((4, 24, 32, 128), jnp.float32),
        pltpu.VMEM((19, 22, 32, 128), jnp.float32),
        pltpu.VMEM((19, 22, 32, 128), jnp.float32),
        pltpu.VMEM((20, 32, 128), jnp.float32),
        pltpu.VMEM((20, 32, 128), jnp.float32),
        pltpu.VMEM((20, 32, 128), jnp.float32),
        pltpu.VMEM((19, 18, 24, 128), jnp.float32),
        pltpu.VMEM((19, 18, 24, 128), jnp.float32),
    ]
    return pl.pallas_call(
        compute,
        out_shape=(f32(16, 16, 128), f32(16, 16, 128), f32(3, 16, 16, 128)),
        scratch_shapes=scratch,
        compiler_params=VMEM,
    )(phase, density, velocity, z_ev, z_od, y_ev, y_od)


def solution(mesh):
    placed = (P("gy", "gz", None), P("gy", "gz", None), P(None, "gy", "gz", None))
    return jax.shard_map(
        shards,
        mesh=mesh,
        in_specs=placed,
        out_specs=placed,
        check_vma=False,
    )
```

time: 118 us -> 36.2 us (0.31)
  the two profiles are of different devices: /device:TPU:102 before, /device:TPU:25 now
where the time goes in v1:
time: 36.2 us; the launch traced here: 36 us
  Pallas kernels  12.5 us (35%)
  starting transfers between devices  10.8 us (30%)
  waiting for transfers between devices  9.25 us (26%)
  local copies, waits for them, and re-layouts  2.8 us (8%)
  between operations  0.66 us (2%)
    pallas_call x1, Pallas kernels, shards(): pl.pallas_call(compute, out_shape=(f32(16, 16, 128), f32(16, 16, 128), f3...  12.3 us
    ppermute x4, starting transfers between devices, swap(): return lax.ppermute(value, axis, pairs)  10.8 us
    ppermute x4, waiting for transfers between devices, swap(): return lax.ppermute(value, axis, pairs)  9.25 us
    unnamed x6, local copies, waits for them, and re-layouts  2.8 us
  transfers between devices with their start and end apart: 4, of which 3 were waited for; matrix products, arithmetic and copies ran while one was open for 0% of the time, Pallas kernels for 0%

profile of v1, /device:TPU:25, one launch (start us, length us, event | category | flops | bytes accessed | tf_op | source)
XLA Modules:
  0.0 36.0 jit_solution(13841540835473072074)
XLA Ops:
  0.6 0.0 copy-start
  0.6 1.0 %copy-done = f32[3,16,16,128]{3,2,1,0:T(8,128)S(1)} copy-done((f32[3,16,16,128]{3,2,1,0:T(8,128)S(1)}, f32[3,16,16,128]{3,2,1,0:T(8,128)}, u32[]{:S(2)}) %copy-start) | copy-done | bytes 393240
  1.6 0.0 copy-start.1
  1.6 0.9 %copy-done.1 = s32[16,16,128]{2,1,0:T(8,128)S(1)} copy-done((s32[16,16,128]{2,1,0:T(8,128)S(1)}, s32[16,16,128]{2,1,0:T(8,128)}, u32[]{:S(2)}) %copy-start.1) | copy-done | bytes 131096
  2.5 0.0 copy-start.2
  2.5 0.9 %copy-done.2 = f32[16,16,128]{2,1,0:T(8,128)S(1)} copy-done((f32[16,16,128]{2,1,0:T(8,128)S(1)}, f32[16,16,128]{2,1,0:T(8,128)}, u32[]{:S(2)}) %copy-start.2) | copy-done | bytes 131096
  3.4 0.1 shard_map.58
  3.5 2.8 %collective-permute-start = (f32[16,16,128]{2,1,0:T(8,128)S(1)}, f32[16,16,128]{2,1,0:T(8,128)S(1)}, u32[]{:S(2)}, u32[]{:S(2)}) collective-permute-start(f32[16,16,128]{2,1,0:T(8,128)S(1)} %get-tuple-element.7), channel_id=1, source_target_pairs={{0,1},{1,0},{2,3},{3,2},{4,5},{5,4},{6,7},{7,6},{8,9},{9,8},{10,11... | collective-permute-start | bytes 393224 | tf_op jit(solution)/shard_map/ppermute | solution.py:395
  6.3 5.5 %collective-permute-start.1 = (f32[16,16,128]{2,1,0:T(8,128)S(1)}, f32[16,16,128]{2,1,0:T(8,128)S(1)}, u32[]{:S(2)}, u32[]{:S(2)}) collective-permute-start(f32[16,16,128]{2,1,0:T(8,128)S(1)} %get-tuple-element.8), channel_id=1, source_target_pairs={{1,2},{2,1},{3,4},{4,3},{5,6},{6,5},{7,8},{8,7},{9,10},{10,9},{11,... | collective-permute-start | bytes 393224 | tf_op jit(solution)/shard_map/ppermute | solution.py:395
  11.8 0.0 collective-permute-done.from_ev.z_ev
  11.9 2.9 %collective-permute-done.1.from_od.z_od = f32[16,16,128]{2,1,0:T(8,128)S(1)} collective-permute-done((f32[16,16,128]{2,1,0:T(8,128)S(1)}, f32[16,16,128]{2,1,0:T(8,128)S(1)}, u32[]{:S(2)}, u32[]{:S(2)}) %collective-permute-start.1) | collective-permute-done | bytes 131104 | tf_op jit(solution)/shard_map/ppermute | solution.py:395
  14.8 0.2 shard_map.59
  14.9 1.6 %collective-permute-start.2 = (f32[16,24,128]{2,1,0:T(8,128)S(1)}, f32[16,24,128]{2,1,0:T(8,128)S(1)}, u32[]{:S(2)}, u32[]{:S(2)}) collective-permute-start(f32[16,24,128]{2,1,0:T(8,128)S(1)} %get-tuple-element.9), channel_id=1, source_target_pairs={{0,16},{16,0},{32,48},{48,32},{64,80},{80,64},{96,112},{112,96},{1... | collective-permute-start | bytes 589832 | tf_op jit(solution)/shard_map/ppermute | solution.py:395
  16.6 0.9 %collective-permute-start.3 = (f32[16,24,128]{2,1,0:T(8,128)S(1)}, f32[16,24,128]{2,1,0:T(8,128)S(1)}, u32[]{:S(2)}, u32[]{:S(2)}) collective-permute-start(f32[16,24,128]{2,1,0:T(8,128)S(1)} %get-tuple-element.10), channel_id=1, source_target_pairs={{16,32},{32,16},{48,64},{64,48},{80,96},{96,80},{112,128},{128,112... | collective-permute-start | bytes 589832 | tf_op jit(solution)/shard_map/ppermute | solution.py:395
  17.4 0.2 collective-permute-done.2.y_ev
  17.6 6.1 %collective-permute-done.3.y_od = f32[16,24,128]{2,1,0:T(8,128)S(1)} collective-permute-done((f32[16,24,128]{2,1,0:T(8,128)S(1)}, f32[16,24,128]{2,1,0:T(8,128)S(1)}, u32[]{:S(2)}, u32[]{:S(2)}) %collective-permute-start.3) | collective-permute-done | bytes 196640 | tf_op jit(solution)/shard_map/ppermute | solution.py:395
  23.8 12.3 %shard_map.60 = (f32[16,16,128]{2,1,0:T(8,128)}, f32[16,16,128]{2,1,0:T(8,128)}, f32[3,16,16,128]{3,2,1,0:T(8,128)}) custom-call(s32[16,16,128]{2,1,0:T(8,128)S(1)} %copy-done.1, f32[16,16,128]{2,1,0:T(8,128)S(1)} %copy-done.2, f32[3,16,16,128]{3,2,1,0:T(8,128)S(1)} %copy-done, f32[16,16,128]{2,1,0:T(8,128)S(1)} %collective-permute-done.from_ev.z_ev, ...), custom_call_target="tpu_custom_call" | custom-call | tf_op jit(solution)/shard_map/pallas_call | solution.py:416
Async XLA Ops:
  0.6 1.0 %copy-start = (f32[3,16,16,128]{3,2,1,0:T(8,128)S(1)}, f32[3,16,16,128]{3,2,1,0:T(8,128)}, u32[]{:S(2)}) copy-start(f32[3,16,16,128]{3,2,1,0:T(8,128)} %velocity.5) | copy-start | bytes 1179652
  1.6 0.9 %copy-start.1 = (s32[16,16,128]{2,1,0:T(8,128)S(1)}, s32[16,16,128]{2,1,0:T(8,128)}, u32[]{:S(2)}) copy-start(s32[16,16,128]{2,1,0:T(8,128)} %phase.5) | copy-start | bytes 393220
  2.5 0.9 %copy-start.2 = (f32[16,16,128]{2,1,0:T(8,128)S(1)}, f32[16,16,128]{2,1,0:T(8,128)}, u32[]{:S(2)}) copy-start(f32[16,16,128]{2,1,0:T(8,128)} %density.5) | copy-start | bytes 393220
  3.5 8.4 %collective-permute-start = (f32[16,16,128]{2,1,0:T(8,128)S(1)}, f32[16,16,128]{2,1,0:T(8,128)S(1)}, u32[]{:S(2)}, u32[]{:S(2)}) collective-permute-start(f32[16,16,128]{2,1,0:T(8,128)S(1)} %get-tuple-element.7), channel_id=1, source_target_pairs={{0,1},{1,0},{2,3},{3,2},{4,5},{5,4},{6,7},{7,6},{8,9},{9,8},{10,11... | collective-permute-start | bytes 393224 | tf_op jit(solution)/shard_map/ppermute | solution.py:395
  6.3 8.4 %collective-permute-start.1 = (f32[16,16,128]{2,1,0:T(8,128)S(1)}, f32[16,16,128]{2,1,0:T(8,128)S(1)}, u32[]{:S(2)}, u32[]{:S(2)}) collective-permute-start(f32[16,16,128]{2,1,0:T(8,128)S(1)} %get-tuple-element.8), channel_id=1, source_target_pairs={{1,2},{2,1},{3,4},{4,3},{5,6},{6,5},{7,8},{8,7},{9,10},{10,9},{11,... | collective-permute-start | bytes 393224 | tf_op jit(solution)/shard_map/ppermute | solution.py:395
  14.9 2.7 %collective-permute-start.2 = (f32[16,24,128]{2,1,0:T(8,128)S(1)}, f32[16,24,128]{2,1,0:T(8,128)S(1)}, u32[]{:S(2)}, u32[]{:S(2)}) collective-permute-start(f32[16,24,128]{2,1,0:T(8,128)S(1)} %get-tuple-element.9), channel_id=1, source_target_pairs={{0,16},{16,0},{32,48},{48,32},{64,80},{80,64},{96,112},{112,96},{1... | collective-permute-start | bytes 589832 | tf_op jit(solution)/shard_map/ppermute | solution.py:395
  16.6 7.2 %collective-permute-start.3 = (f32[16,24,128]{2,1,0:T(8,128)S(1)}, f32[16,24,128]{2,1,0:T(8,128)S(1)}, u32[]{:S(2)}, u32[]{:S(2)}) collective-permute-start(f32[16,24,128]{2,1,0:T(8,128)S(1)} %get-tuple-element.10), channel_id=1, source_target_pairs={{16,32},{32,16},{48,64},{64,48},{80,96},{96,80},{112,128},{128,112... | collective-permute-start | bytes 589832 | tf_op jit(solution)/shard_map/ppermute | solution.py:395

commit v2 on v1

v2 whole, which is shorter than its diff:
```python
import math

import jax
import jax.numpy as jnp
from jax import lax
from jax.experimental import pallas as pl
from jax.experimental.pallas import tpu as pltpu
from jax.sharding import PartitionSpec as P

VELOCITIES = [
    [0, 0, 0],
    [1, 0, 0],
    [-1, 0, 0],
    [0, 1, 0],
    [0, -1, 0],
    [0, 0, 1],
    [0, 0, -1],
    [1, 1, 0],
    [-1, -1, 0],
    [1, -1, 0],
    [-1, 1, 0],
    [1, 0, 1],
    [-1, 0, -1],
    [1, 0, -1],
    [-1, 0, 1],
    [0, 1, 1],
    [0, -1, -1],
    [0, 1, -1],
    [0, -1, 1],
]
INDEX = {tuple(v): i for i, v in enumerate(VELOCITIES)}
relax_time = 0.8
surface_amp = 0.05
recolouring_strength = 0.7
grad_floor = 0.05


def vmem(mib):
    return pltpu.CompilerParams(vmem_limit_bytes=mib * 1024 * 1024)


def rolled(value, shift):
    return pltpu.roll(value, shift % 128, 1) if shift else value


def depth(at):
    return 4 if at == 4 else 3


def fill_z(msg, low, phase, density, velocity):
    for at in range(5):
        n = depth(at)
        start = 0 if low else 16 - n
        if at == 0:
            msg[:, 0:3, :] = density[:, start : start + n, :]
        elif at == 4:
            msg[:, 12:16, :] = phase[:, start : start + n, :].astype(jnp.float32)
        else:
            msg[:, 3 * at : 3 * at + n, :] = velocity[at - 1, :, start : start + n, :]


def fill_y(msg, low, phase, density, velocity):
    for at in range(5):
        for k in range(depth(at)):
            y = k if low else 16 - depth(at) + k
            msg[3 * at + k] = own_plane(at, y, phase, density, velocity)


def own_plane(at, y, phase, density, velocity):
    if at == 0:
        return density[y]
    if at == 4:
        return phase[y].astype(jnp.float32)
    return velocity[at - 1, y]


def is_odd(axis):
    return lax.rem(lax.axis_index(axis), 2) == 1


def either(odd, work):
    @pl.when(odd)
    def _():
        work(True)

    @pl.when(jnp.logical_not(odd))
    def _():
        work(False)


def pack_own(phase_in, density_in, velocity_in, phase, density, velocity, z_ev, z_od, y_ev, y_od, sems):
    copies = [
        pltpu.make_async_copy(velocity_in, velocity, sems.at[0]),
        pltpu.make_async_copy(density_in, density, sems.at[1]),
        pltpu.make_async_copy(phase_in, phase, sems.at[2]),
    ]
    for c in copies:
        c.start()
    for c in copies:
        c.wait()
    own = (phase, density, velocity)

    def along_z(odd):
        fill_z(z_ev, odd, *own)
        fill_z(z_od, not odd, *own)

    def along_y(odd):
        fill_y(y_ev, odd, *own)
        fill_y(y_od, not odd, *own)

    either(is_odd("gz"), along_z)
    either(is_odd("gy"), along_y)


def pack_corners(from_ev, from_od, msg_ev, msg_od):
    odd_y = is_odd("gy")

    def fill(msg, low, z_low, z_high):
        for at in range(5):
            n = depth(at)
            for k in range(n):
                y = k if low else 16 - n + k
                row = 3 * at + k
                if n == 3:
                    msg[row] = jnp.zeros((8, 128), jnp.float32)
                msg[row, 4 - n : 4, :] = z_low[y, 3 * at : 3 * at + n, :]
                msg[row, 4 : 4 + n, :] = z_high[y, 3 * at : 3 * at + n, :]

    def along_z(odd_z):
        z_low, z_high = (from_ev, from_od) if odd_z else (from_od, from_ev)

        def along_y(odd):
            fill(msg_ev, odd, z_low, z_high)
            fill(msg_od, not odd, z_low, z_high)

        either(odd_y, along_y)

    either(is_odd("gz"), along_z)


W2 = 1.0 / 36.0
GAIN = 1.0 / relax_time
LEFT = 1.0 - GAIN


def gradient(load):
    near, far = 6.0 / 18.0, 6.0 / 36.0
    mid = load(0, 0)
    up_y, down_y, up_z, down_z = load(1, 0), load(-1, 0), load(0, 1), load(0, -1)
    pp, pm, mp, mm = load(1, 1), load(1, -1), load(-1, 1), load(-1, -1)
    along_x = near * mid + far * ((up_y + down_y) + (up_z + down_z))
    diff_y = up_y - down_y
    diff_z = up_z - down_z
    cross = pp - mm
    other = pm - mp
    grad_x = rolled(along_x, -1) - rolled(along_x, 1)
    grad_y = near * diff_y + far * ((cross + other) + (rolled(diff_y, 1) + rolled(diff_y, -1)))
    grad_z = near * diff_z + far * ((cross - other) + (rolled(diff_z, 1) + rolled(diff_z, -1)))
    return grad_x, grad_y, grad_z


def collide(level, rest, tensor, flow, step, share, tail, store_post, store_red):
    def emit(c, post, recolour):
        i = INDEX[c]
        if tail is not None:
            post = post + tail[i]
        red = share * post
        if recolour is not None:
            red = red + recolour
        store_post(i, post)
        store_red(i, red)

    emit((0, 0, 0), rest, None)
    xx, yy, zz, xy, xz, yz = tensor
    diag = (xx, yy, zz)
    lev = [level + d for d in diag]
    for axis in range(3):
        even = lev[axis] + lev[axis]
        odd = flow[axis] + flow[axis]
        recolour = step[axis] + step[axis]
        c = [0, 0, 0]
        c[axis] = 1
        emit(tuple(c), even + odd, recolour)
        c[axis] = -1
        emit(tuple(c), even - odd, -recolour)
    slant = [s * (1.0 / math.sqrt(2.0)) for s in step]
    for a, b, cross in ((0, 1, xy), (0, 2, xz), (1, 2, yz)):
        base = lev[a] + diag[b]
        twice = cross + cross
        for sign in (1, -1):
            even = base + twice if sign > 0 else base - twice
            odd = flow[a] + flow[b] if sign > 0 else flow[a] - flow[b]
            recolour = slant[a] + slant[b] if sign > 0 else slant[a] - slant[b]
            c = [0, 0, 0]
            c[a], c[b] = 1, sign
            emit(tuple(c), even + odd, recolour)
            emit(tuple(-v for v in c), even - odd, -recolour)


def surface(grad):
    square = grad[0] * grad[0] + grad[1] * grad[1] + grad[2] * grad[2]
    root = lax.rsqrt(jnp.maximum(square, 1e-30))
    return square * root, jnp.minimum(root, 1.0 / grad_floor)


def products(vec, other):
    x, y, z = vec
    p, q, r = other
    return [x * p, y * q, z * r, x * q, x * r, y * r]


def step_one(label, dens, vel, grad, store_post, store_red):
    scale = LEFT * W2
    mix = label * (1.0 - label) * dens
    gmag, inv = surface(grad)
    speed = vel[0] * vel[0] + vel[1] * vel[1] + vel[2] * vel[2]
    scaled = scale * dens

    def relax(pop, eq):
        return pop - (pop - eq) * GAIN

    rest = scaled - 1.5 * scaled * speed
    rest = relax(rest, rest)
    flow = [(3.0 * scaled) * v for v in vel]
    flow = [relax(v, v) for v in flow]
    tensor = products([1.5 * f for f in flow], vel)
    pull = (0.5 * surface_amp * scale) * inv
    tensor = [t + s for t, s in zip(tensor, products([pull * g for g in grad], grad))]
    gm = (0.5 * surface_amp * scale) * gmag
    h = (recolouring_strength * scale) * mix * inv
    collide(rest - gm, 12.0 * (rest + gm), tensor, flow, [h * g for g in grad], label, None, store_post, store_red)


def moment(pops, a):
    total = None
    for i, c in enumerate(VELOCITIES):
        if c[a]:
            term = pops[i]
            total = (term if c[a] > 0 else -term) if total is None else (total + term if c[a] > 0 else total - term)
    return total


def step_two(rho, rinv, share, tail, grad, store_post, store_red):
    mix = share * (1.0 - share) * rho
    gmag, inv = surface(grad)
    scaled = [moment(tail, a) for a in range(3)]
    vel = [(rinv * (1.0 / LEFT)) * m for m in scaled]
    flow = [(3.0 * GAIN * W2 / LEFT) * m for m in scaled]
    tensor = products([1.5 * f for f in flow], vel)
    rest = (GAIN * W2) * rho - (1.0 / 3.0) * (tensor[0] + tensor[1] + tensor[2])
    pull = (0.5 * surface_amp * W2) * inv
    tensor = [t + s for t, s in zip(tensor, products([pull * g for g in grad], grad))]
    gm = (0.5 * surface_amp * W2) * gmag
    h = (recolouring_strength * W2) * mix * inv
    collide(rest - gm, 12.0 * (rest + gm), tensor, flow, [h * g for g in grad], share, tail, store_post, store_red)


def streamed_parts(load, weight=None):
    parts = {0: [], 1: [], -1: []}
    for i, c in enumerate(VELOCITIES):
        w = 1 if weight is None else c[weight]
        if w:
            parts[c[0]].append((load(i), w))

    def tree(terms):
        while len(terms) > 1:
            joined = []
            for (a, wa), (b, wb) in zip(terms[::2], terms[1::2]):
                if wa == wb:
                    joined.append((a + b, wa))
                elif wa > 0:
                    joined.append((a - b, 1))
                else:
                    joined.append((b - a, 1))
            terms = joined + terms[len(terms) & ~1 :]
        value, w = terms[0]
        return value if w > 0 else -value

    return {s: tree(terms) if terms else None for s, terms in parts.items()}


def joined(parts):
    side = rolled(parts[1], 1) + rolled(parts[-1], -1)
    return side if parts[0] is None else parts[0] + side


def pass_a(refs, j, k):
    label, raw, post1, red1 = refs["label"], refs["raw"], refs["post1"], refs["red1"]
    grad = gradient(lambda dy, dz: label[j + 1 + dy, 1 + dz + k : 9 + dz + k, :])
    tile = lambda at: raw[at, j + 1, 1 + k : 9 + k, :]

    def store_post(i, v):
        post1[i, j, k : k + 8, :] = v

    def store_red(i, v):
        red1[i, j, k : k + 8, :] = v

    step_one(label[j + 1, 1 + k : 9 + k, :], tile(0), [tile(1), tile(2), tile(3)], grad, store_post, store_red)


def pass_b(refs, j, k):
    def total(ref):
        def load(i):
            _, cy, cz = VELOCITIES[i]
            return ref[i, j + 1 - cy, 1 - cz + k : 9 - cz + k, :]

        return joined(streamed_parts(load)) * (1.0 / LEFT)

    rho = total(refs["post1"])
    rinv = 1.0 / rho
    refs["rho_s"][j, k : k + 8, :] = rho
    refs["rinv_s"][j, k : k + 8, :] = rinv
    refs["share_s"][j, k : k + 8, :] = total(refs["red1"]) * rinv


def pass_c(refs, j, k):
    post1, post2, red2, share = refs["post1"], refs["post2"], refs["red2"], refs["share_s"]
    tail = []
    for i, (cx, cy, cz) in enumerate(VELOCITIES):
        tail.append(rolled(post1[i, j + 2 - cy, 2 - cz + k : 10 - cz + k, :], cx))
    grad = gradient(lambda dy, dz: share[j + 1 + dy, 1 + dz + k : 9 + dz + k, :])
    tile = lambda ref: ref[j + 1, 1 + k : 9 + k, :]

    def store_post(i, v):
        post2[i, j, k : k + 8, :] = v

    def store_red(i, v):
        red2[i, j, k : k + 8, :] = v

    step_two(tile(refs["rho_s"]), tile(refs["rinv_s"]), tile(share), tail, grad, store_post, store_red)


def pass_d(refs, j, k, store):
    def load_of(ref):
        held = {}

        def load(i):
            if i not in held:
                _, cy, cz = VELOCITIES[i]
                held[i] = ref[i, j + 1 - cy, 1 - cz + k : 9 - cz + k, :]
            return held[i]

        return load

    load = load_of(refs["post2"])
    parts = streamed_parts(load)
    up, down = rolled(parts[1], 1), rolled(parts[-1], -1)
    rho = parts[0] + (up + down)
    red = joined(streamed_parts(load_of(refs["red2"])))
    store(j, k, [red, rho - red, up - down, joined(streamed_parts(load, 1)), joined(streamed_parts(load, 2))])


def sweep(work, refs, rows, chunks, unroll):
    count = rows[0][1] - rows[0][0]

    def body(t, carry):
        for start, _ in rows:
            for k in chunks:
                work(refs, start + t, k)
        return carry

    lax.fori_loop(0, count, body, 0, unroll=unroll)


STATE = dict(
    label=(24, 32, 128),
    raw=(4, 24, 32, 128),
    post1=(19, 22, 32, 128),
    red1=(19, 22, 32, 128),
    rho_s=(20, 32, 128),
    rinv_s=(20, 32, 128),
    share_s=(20, 32, 128),
    post2=(19, 18, 24, 128),
    red2=(19, 18, 24, 128),
)
NAMES = list(STATE)
A_Z, B_Z, C_Z, D_Z = (0, 8, 16), (0, 8, 14), (0, 8, 12), (0, 8)


def frame_of(refs, at):
    return refs["label"] if at == 4 else refs["raw"].at[at]


def inner(phase, density, velocity, z_ev, z_od, y_ev, y_od, *rest):
    refs = dict(zip(NAMES, rest))
    done = rest[len(NAMES)]

    def assemble(odd):
        low, high = (z_ev, z_od) if odd else (z_od, z_ev)

        def body(y, carry):
            for at in range(5):
                ref, n = frame_of(refs, at), depth(at)
                ref[y + 4, 4:20, :] = own_plane(at, y, phase, density, velocity)
                ref[y + 4, 4 - n : 4, :] = low[y, 3 * at : 3 * at + n, :]
                ref[y + 4, 20 : 20 + n, :] = high[y, 3 * at : 3 * at + n, :]
            return carry

        lax.fori_loop(0, 16, body, 0, unroll=2)

    def beside(odd):
        low, high = (y_ev, y_od) if odd else (y_od, y_ev)
        for at in range(5):
            ref, n = frame_of(refs, at), depth(at)
            for k in range(n):
                ref[4 - n + k, 4:20, :] = low[3 * at + k]
                ref[20 + k, 4:20, :] = high[3 * at + k]

    either(is_odd("gz"), assemble)
    either(is_odd("gy"), beside)

    def store(j, k, values):
        for at, v in enumerate(values):
            done[at, j - 4, k : k + 8, :] = v

    sweep(pass_a, refs, [(4, 18)], A_Z, 2)
    sweep(pass_a, refs, [(0, 4), (18, 22)], A_Z[1:2], 2)
    sweep(pass_b, refs, [(4, 16)], B_Z, 2)
    sweep(pass_b, refs, [(0, 4), (16, 20)], B_Z[1:2], 2)
    sweep(pass_c, refs, [(4, 14)], C_Z, 2)
    sweep(pass_c, refs, [(0, 4), (14, 18)], C_Z[1:2], 2)
    sweep(lambda r, j, k: pass_d(r, j, k, store), refs, [(4, 12)], D_Z, 2)


def outer(y_ev, y_od, done, *rest):
    n = len(NAMES)
    refs = dict(zip(NAMES, rest[n : 2 * n]))
    out_red, out_blue, out_mom, edge, sems = rest[2 * n :]

    def send(src, rows, at_rows, sem):
        outs = [out_red, out_blue, out_mom.at[0], out_mom.at[1], out_mom.at[2]]
        return [pltpu.make_async_copy(src.at[f, pl.ds(rows, at_rows[1])], outs[f].at[pl.ds(at_rows[0], at_rows[1])], sems.at[sem, f]) for f in range(5)]

    first = send(done, 0, (4, 8), 0)
    for c in first:
        c.start()

    def corners(odd):
        low, high = (y_ev, y_od) if odd else (y_od, y_ev)
        for at in range(5):
            ref, d = frame_of(refs, at), depth(at)
            for k in range(d):
                for row, msg in ((4 - d + k, low), (20 + k, high)):
                    ref[row, 4 - d : 4, :] = msg[3 * at + k, 4 - d : 4, :]
                    ref[row, 20 : 20 + d, :] = msg[3 * at + k, 4 : 4 + d, :]

    either(is_odd("gy"), corners)

    def store_low(j, k, values):
        for at, v in enumerate(values):
            edge[at, j, k : k + 8, :] = v

    def store_high(j, k, values):
        for at, v in enumerate(values):
            edge[at, j - 8, k : k + 8, :] = v

    sweep(pass_a, refs, [(0, 4), (18, 22)], A_Z[::2], 2)
    sweep(pass_b, refs, [(0, 4), (16, 20)], B_Z[::2], 2)
    sweep(pass_c, refs, [(0, 4), (14, 18)], C_Z[::2], 2)

    def last(r, t, k):
        pass_d(r, t, k, store_low)
        pass_d(r, t + 12, k, store_high)

    sweep(last, refs, [(0, 4)], D_Z, 2)
    second = send(edge, 0, (0, 4), 1) + send(edge, 4, (12, 4), 2)
    for c in second:
        c.start()
    for c in first + second:
        c.wait()


def f32(*shape):
    return jax.ShapeDtypeStruct(shape, jnp.float32)


def swap(value, axis, first):
    count = lax.axis_size(axis)
    pairs = []
    for low in range(first, count, 2):
        high = (low + 1) % count
        pairs += [(low, high), (high, low)]
    return lax.ppermute(value, axis, pairs)


def shards(phase, density, velocity):
    in_vmem = pl.BlockSpec(memory_space=pltpu.VMEM)
    in_hbm = pl.BlockSpec(memory_space=pltpu.HBM)
    state = [f32(*s) for s in STATE.values()]
    phase, density, velocity, z_ev, z_od, y_ev, y_od = pl.pallas_call(
        pack_own,
        out_shape=(jax.ShapeDtypeStruct((16, 16, 128), jnp.int32), f32(16, 16, 128), f32(3, 16, 16, 128)) + (f32(16, 16, 128),) * 4,
        in_specs=[in_hbm] * 3,
        out_specs=(in_vmem,) * 7,
        scratch_shapes=[pltpu.SemaphoreType.DMA((3,))],
        compiler_params=vmem(8),
    )(phase, density, velocity)
    z_od = swap(z_od, "gz", 1)
    z_ev = swap(z_ev, "gz", 0)
    y_od = swap(y_od, "gy", 1)
    y_ev = swap(y_ev, "gy", 0)
    c_ev, c_od = pl.pallas_call(pack_corners, out_shape=(f32(16, 8, 128),) * 2, compiler_params=vmem(4))(z_ev, z_od)
    c_od = swap(c_od, "gy", 1)
    c_ev = swap(c_ev, "gy", 0)
    made = pl.pallas_call(
        inner,
        out_shape=tuple(state) + (f32(5, 8, 16, 128),),
        compiler_params=vmem(8),
        cost_estimate=pl.CostEstimate(flops=40_000_000, bytes_accessed=20_000_000, transcendentals=0),
    )(phase, density, velocity, z_ev, z_od, y_ev, y_od)
    n = len(NAMES)
    return pl.pallas_call(
        outer,
        out_shape=tuple(state) + (f32(16, 16, 128), f32(16, 16, 128), f32(3, 16, 16, 128)),
        in_specs=[in_vmem] * (3 + n),
        out_specs=(in_vmem,) * n + (in_hbm,) * 3,
        scratch_shapes=[pltpu.VMEM((5, 8, 16, 128), jnp.float32), pltpu.SemaphoreType.DMA((3, 5))],
        input_output_aliases={3 + i: i for i in range(n)},
        compiler_params=vmem(8),
    )(c_ev, c_od, made[n], *made[:n])[n:]


def solution(mesh):
    placed = (P("gy", "gz", None), P("gy", "gz", None), P(None, "gy", "gz", None))
    return jax.shard_map(
        shards,
        mesh=mesh,
        in_specs=placed,
        out_specs=placed,
        check_vma=False,
    )
```

time: 36.2 us -> 28.8 us (0.80)
  the two profiles are of different devices: /device:TPU:25 before, /device:TPU:27 now
where the time goes in v2:
time: 28.8 us; the launch traced here: 28.6 us
  starting transfers between devices  12 us (42%)
  Pallas kernels  9.09 us (32%)
  waiting for transfers between devices  4.08 us (14%)
  local copies, waits for them, and re-layouts  2.8 us (10%)
  between operations  0.68 us (2%)
    ppermute x6, starting transfers between devices, swap(): return lax.ppermute(value, axis, pairs)  12 us
    pallas_call x1, Pallas kernels, shards(): pl.pallas_call(inner, out_shape=tuple(state) + (f32(5, 8, 16, 128),), com...  5.63 us
    ppermute x6, waiting for transfers between devices, swap(): return lax.ppermute(value, axis, pairs)  4.08 us
    unnamed x6, local copies, waits for them, and re-layouts  2.8 us
    pallas_call x1, Pallas kernels, shards(): pl.pallas_call(outer, out_shape=tuple(state) + (f32(16, 16, 128), f32(16,...  2.79 us
    pallas_call x1, Pallas kernels, shards(): pl.pallas_call(pack_own, out_shape=(jax.ShapeDtypeStruct((16, 16, 128), j...  0.65 us
  transfers between devices with their start and end apart: 6, of which 2 were waited for; matrix products, arithmetic and copies ran while one was open for 0% of the time, Pallas kernels for 20%

profile of v2, /device:TPU:27, one launch (start us, length us, event | category | flops | bytes accessed | tf_op | source)
XLA Modules:
  0.0 28.6 jit_solution(2049332055071866805)
XLA Ops:
  0.6 0.0 copy-start
  0.6 1.0 %copy-done = f32[3,16,16,128]{3,2,1,0:T(8,128)S(1)} copy-done((f32[3,16,16,128]{3,2,1,0:T(8,128)S(1)}, f32[3,16,16,128]{3,2,1,0:T(8,128)}, u32[]{:S(2)}) %copy-start) | copy-done | bytes 393240
  1.6 0.0 copy-start.1
  1.6 0.9 %copy-done.1 = s32[16,16,128]{2,1,0:T(8,128)S(1)} copy-done((s32[16,16,128]{2,1,0:T(8,128)S(1)}, s32[16,16,128]{2,1,0:T(8,128)}, u32[]{:S(2)}) %copy-start.1) | copy-done | bytes 131096
  2.5 0.0 copy-start.2
  2.5 0.9 %copy-done.2 = f32[16,16,128]{2,1,0:T(8,128)S(1)} copy-done((f32[16,16,128]{2,1,0:T(8,128)S(1)}, f32[16,16,128]{2,1,0:T(8,128)}, u32[]{:S(2)}) %copy-start.2) | copy-done | bytes 131096
  3.4 0.6 %shard_map.58 = (s32[16,16,128]{2,1,0:T(8,128)S(1)}, f32[16,16,128]{2,1,0:T(8,128)S(1)}, f32[3,16,16,128]{3,2,1,0:T(8,128)S(1)}, f32[16,16,128]{2,1,0:T(8,128)S(...) custom-call(s32[16,16,128]{2,1,0:T(8,128)S(1)} %copy-done.1, ...), custom_call_target="tpu_custom_call" | custom-call | tf_op jit(solution)/shard_map/pallas_call | solution.py:490
  4.1 1.9 %collective-permute-start = (f32[16,16,128]{2,1,0:T(8,128)S(1)}, f32[16,16,128]{2,1,0:T(8,128)S(1)}, u32[]{:S(2)}, u32[]{:S(2)}) collective-permute-start(f32[16,16,128]{2,1,0:T(8,128)S(1)} %get-tuple-element.25), channel_id=1, source_target_pairs={{0,1},{1,0},{2,3},{3,2},{4,5},{5,4},{6,7},{7,6},{8,9},{9,8},{10,11... | collective-permute-start | bytes 393224 | tf_op jit(solution)/shard_map/ppermute | solution.py:483
  6.0 6.4 %collective-permute-start.1 = (f32[16,16,128]{2,1,0:T(8,128)S(1)}, f32[16,16,128]{2,1,0:T(8,128)S(1)}, u32[]{:S(2)}, u32[]{:S(2)}) collective-permute-start(f32[16,16,128]{2,1,0:T(8,128)S(1)} %get-tuple-element.26), channel_id=1, source_target_pairs={{1,2},{2,1},{3,4},{4,3},{5,6},{6,5},{7,8},{8,7},{9,10},{10,9},{11,... | collective-permute-start | bytes 393224 | tf_op jit(solution)/shard_map/ppermute | solution.py:483
  12.4 1.2 %collective-permute-start.4 = (f32[16,16,128]{2,1,0:T(8,128)S(1)}, f32[16,16,128]{2,1,0:T(8,128)S(1)}, u32[]{:S(2)}, u32[]{:S(2)}) collective-permute-start(f32[16,16,128]{2,1,0:T(8,128)S(1)} %get-tuple-element.32), channel_id=1, source_target_pairs={{0,16},{16,0},{32,48},{48,32},{64,80},{80,64},{96,112},{112,96},{1... | collective-permute-start | bytes 393224 | tf_op jit(solution)/shard_map/ppermute | solution.py:483
  13.7 0.0 collective-permute-start.5
  13.7 0.0 collective-permute-done.from_ev.z_ev
  13.7 1.7 %collective-permute-done.1.from_od.z_od = f32[16,16,128]{2,1,0:T(8,128)S(1)} collective-permute-done((f32[16,16,128]{2,1,0:T(8,128)S(1)}, f32[16,16,128]{2,1,0:T(8,128)S(1)}, u32[]{:S(2)}, u32[]{:S(2)}) %collective-permute-start.1) | collective-permute-done | bytes 131104 | tf_op jit(solution)/shard_map/ppermute | solution.py:483
  15.4 1.7 %collective-permute-start.2 = (f32[16,8,128]{2,1,0:T(8,128)S(1)}, f32[16,8,128]{2,1,0:T(8,128)S(1)}, u32[]{:S(2)}, u32[]{:S(2)}) collective-permute-start(f32[16,8,128]{2,1,0:T(8,128)S(1)} %get-tuple-element.27), channel_id=1, source_target_pairs={{0,16},{16,0},{32,48},{48,32},{64,80},{80,64},{96,112},{112,96},{1... | collective-permute-start | bytes 196616 | tf_op jit(solution)/shard_map/ppermute | solution.py:483
  17.1 0.6 %collective-permute-start.3 = (f32[16,8,128]{2,1,0:T(8,128)S(1)}, f32[16,8,128]{2,1,0:T(8,128)S(1)}, u32[]{:S(2)}, u32[]{:S(2)}) collective-permute-start(f32[16,8,128]{2,1,0:T(8,128)S(1)} %get-tuple-element.28), channel_id=1, source_target_pairs={{16,32},{32,16},{48,64},{64,48},{80,96},{96,80},{112,128},{128,112... | collective-permute-start | bytes 196616 | tf_op jit(solution)/shard_map/ppermute | solution.py:483
  17.8 0.0 collective-permute-done.4.y_ev
  17.8 2.4 %collective-permute-done.5.y_od = f32[16,16,128]{2,1,0:T(8,128)S(1)} collective-permute-done((f32[16,16,128]{2,1,0:T(8,128)S(1)}, f32[16,16,128]{2,1,0:T(8,128)S(1)}, u32[]{:S(2)}, u32[]{:S(2)}) %collective-permute-start.5) | collective-permute-done | bytes 131104 | tf_op jit(solution)/shard_map/ppermute | solution.py:483
  20.2 5.6 %shard_map.60 = (f32[24,32,128]{2,1,0:T(8,128)S(1)}, f32[4,24,32,128]{3,2,1,0:T(8,128)S(1)}, f32[19,22,32,128]{3,2,1,0:T(8,128)S(1)}, f32[19,22,32,128]{3,2,1,0:...) custom-call(s32[16,16,128]{2,1,0:T(8,128)S(1)} %get-tuple-element.29, ...), custom_call_target="tpu_custom_call" | custom-call | flops 40000000 | bytes 20000000 | tf_op jit(solution)/shard_map/pallas_call | solution.py:505
  25.8 0.0 collective-permute-done.2.y_ev
  25.8 0.0 collective-permute-done.3.y_od
  25.8 2.8 %shard_map.61 = (f32[24,32,128]{2,1,0:T(8,128)S(1)}, f32[4,24,32,128]{3,2,1,0:T(8,128)S(1)}, f32[19,22,32,128]{3,2,1,0:T(8,128)S(1)}, f32[19,22,32,128]{3,2,1,0:...) custom-call(f32[16,8,128]{2,1,0:T(8,128)S(1)} %collective-permute-do, ...), custom_call_target="tpu_custom_call", output_to_operand_aliasing={{0}: (3, {}), {1}: (4, {}), {2}: (5, {}), {3}: (6, {}), {4}... | custom-call | tf_op jit(solution)/shard_map/pallas_call | solution.py:512
  (1 shorter events, 0.0 us)
Async XLA Ops:
  0.6 1.0 %copy-start = (f32[3,16,16,128]{3,2,1,0:T(8,128)S(1)}, f32[3,16,16,128]{3,2,1,0:T(8,128)}, u32[]{:S(2)}) copy-start(f32[3,16,16,128]{3,2,1,0:T(8,128)} %velocity_in.1) | copy-start | bytes 1179652
  1.6 0.9 %copy-start.1 = (s32[16,16,128]{2,1,0:T(8,128)S(1)}, s32[16,16,128]{2,1,0:T(8,128)}, u32[]{:S(2)}) copy-start(s32[16,16,128]{2,1,0:T(8,128)} %phase_in.1) | copy-start | bytes 393220
  2.5 0.9 %copy-start.2 = (f32[16,16,128]{2,1,0:T(8,128)S(1)}, f32[16,16,128]{2,1,0:T(8,128)}, u32[]{:S(2)}) copy-start(f32[16,16,128]{2,1,0:T(8,128)} %density_in.1) | copy-start | bytes 393220
  4.1 9.6 %collective-permute-start = (f32[16,16,128]{2,1,0:T(8,128)S(1)}, f32[16,16,128]{2,1,0:T(8,128)S(1)}, u32[]{:S(2)}, u32[]{:S(2)}) collective-permute-start(f32[16,16,128]{2,1,0:T(8,128)S(1)} %get-tuple-element.25), channel_id=1, source_target_pairs={{0,1},{1,0},{2,3},{3,2},{4,5},{5,4},{6,7},{7,6},{8,9},{9,8},{10,11... | collective-permute-start | bytes 393224 | tf_op jit(solution)/shard_map/ppermute | solution.py:483
  6.0 9.3 %collective-permute-start.1 = (f32[16,16,128]{2,1,0:T(8,128)S(1)}, f32[16,16,128]{2,1,0:T(8,128)S(1)}, u32[]{:S(2)}, u32[]{:S(2)}) collective-permute-start(f32[16,16,128]{2,1,0:T(8,128)S(1)} %get-tuple-element.26), channel_id=1, source_target_pairs={{1,2},{2,1},{3,4},{4,3},{5,6},{6,5},{7,8},{8,7},{9,10},{10,9},{11,... | collective-permute-start | bytes 393224 | tf_op jit(solution)/shard_map/ppermute | solution.py:483
  12.4 5.3 %collective-permute-start.4 = (f32[16,16,128]{2,1,0:T(8,128)S(1)}, f32[16,16,128]{2,1,0:T(8,128)S(1)}, u32[]{:S(2)}, u32[]{:S(2)}) collective-permute-start(f32[16,16,128]{2,1,0:T(8,128)S(1)} %get-tuple-element.32), channel_id=1, source_target_pairs={{0,16},{16,0},{32,48},{48,32},{64,80},{80,64},{96,112},{112,96},{1... | collective-permute-start | bytes 393224 | tf_op jit(solution)/shard_map/ppermute | solution.py:483
  13.7 6.5 %collective-permute-start.5 = (f32[16,16,128]{2,1,0:T(8,128)S(1)}, f32[16,16,128]{2,1,0:T(8,128)S(1)}, u32[]{:S(2)}, u32[]{:S(2)}) collective-permute-start(f32[16,16,128]{2,1,0:T(8,128)S(1)} %get-tuple-element.33), channel_id=1, source_target_pairs={{16,32},{32,16},{48,64},{64,48},{80,96},{96,80},{112,128},{128,112... | collective-permute-start | bytes 393224 | tf_op jit(solution)/shard_map/ppermute | solution.py:483
  15.4 10.4 %collective-permute-start.2 = (f32[16,8,128]{2,1,0:T(8,128)S(1)}, f32[16,8,128]{2,1,0:T(8,128)S(1)}, u32[]{:S(2)}, u32[]{:S(2)}) collective-permute-start(f32[16,8,128]{2,1,0:T(8,128)S(1)} %get-tuple-element.27), channel_id=1, source_target_pairs={{0,16},{16,0},{32,48},{48,32},{64,80},{80,64},{96,112},{112,96},{1... | collective-permute-start | bytes 196616 | tf_op jit(solution)/shard_map/ppermute | solution.py:483
  17.1 8.7 %collective-permute-start.3 = (f32[16,8,128]{2,1,0:T(8,128)S(1)}, f32[16,8,128]{2,1,0:T(8,128)S(1)}, u32[]{:S(2)}, u32[]{:S(2)}) collective-permute-start(f32[16,8,128]{2,1,0:T(8,128)S(1)} %get-tuple-element.28), channel_id=1, source_target_pairs={{16,32},{32,16},{48,64},{64,48},{80,96},{96,80},{112,128},{128,112... | collective-permute-start | bytes 196616 | tf_op jit(solution)/shard_map/ppermute | solution.py:483

commit v3 on v2

--- a/solution.py
+++ b/solution.py
@@ -143,11 +143,11 @@
 LEFT = 1.0 - GAIN
 
 
-def gradient(load):
+def gradient(q):
     near, far = 6.0 / 18.0, 6.0 / 36.0
-    mid = load(0, 0)
-    up_y, down_y, up_z, down_z = load(1, 0), load(-1, 0), load(0, 1), load(0, -1)
-    pp, pm, mp, mm = load(1, 1), load(1, -1), load(-1, 1), load(-1, -1)
+    mid = q[0, 0]
+    up_y, down_y, up_z, down_z = q[1, 0], q[-1, 0], q[0, 1], q[0, -1]
+    pp, pm, mp, mm = q[1, 1], q[1, -1], q[-1, 1], q[-1, -1]
     along_x = near * mid + far * ((up_y + down_y) + (up_z + down_z))
     diff_y = up_y - down_y
     diff_z = up_z - down_z
@@ -159,42 +159,33 @@
     return grad_x, grad_y, grad_z
 
 
-def collide(level, rest, tensor, flow, step, share, tail, store_post, store_red):
-    def emit(c, post, recolour):
-        i = INDEX[c]
-        if tail is not None:
-            post = post + tail[i]
-        red = share * post
-        if recolour is not None:
-            red = red + recolour
-        store_post(i, post)
-        store_red(i, red)
-
-    emit((0, 0, 0), rest, None)
+def collide(level, rest, tensor, flow, step, share, tail):
+    def left(c, post):
+        return post if tail is None else post + tail[INDEX[c]]
+
+    def pair(c, even, odd, recolour):
+        back = tuple(-v for v in c)
+        post = left(c, even + odd)
+        yield INDEX[c], post, share * post + recolour
+        post = left(back, even - odd)
+        yield INDEX[back], post, share * post - recolour
+
+    post = left((0, 0, 0), rest)
+    yield 0, post, share * post
     xx, yy, zz, xy, xz, yz = tensor
     diag = (xx, yy, zz)
     lev = [level + d for d in diag]
     for axis in range(3):
-        even = lev[axis] + lev[axis]
-        odd = flow[axis] + flow[axis]
-        recolour = step[axis] + step[axis]
-        c = [0, 0, 0]
-        c[axis] = 1
-        emit(tuple(c), even + odd, recolour)
-        c[axis] = -1
-        emit(tuple(c), even - odd, -recolour)
+        c = tuple(int(a == axis) for a in range(3))
+        yield from pair(c, lev[axis] + lev[axis], flow[axis] + flow[axis], step[axis] + step[axis])
     slant = [s * (1.0 / math.sqrt(2.0)) for s in step]
     for a, b, cross in ((0, 1, xy), (0, 2, xz), (1, 2, yz)):
         base = lev[a] + diag[b]
         twice = cross + cross
-        for sign in (1, -1):
-            even = base + twice if sign > 0 else base - twice
-            odd = flow[a] + flow[b] if sign > 0 else flow[a] - flow[b]
-            recolour = slant[a] + slant[b] if sign > 0 else slant[a] - slant[b]
-            c = [0, 0, 0]
-            c[a], c[b] = 1, sign
-            emit(tuple(c), even + odd, recolour)
-            emit(tuple(-v for v in c), even - odd, -recolour)
+        c = tuple(int(v in (a, b)) for v in range(3))
+        yield from pair(c, base + twice, flow[a] + flow[b], slant[a] + slant[b])
+        c = tuple(int(v == a) - int(v == b) for v in range(3))
+        yield from pair(c, base - twice, flow[a] - flow[b], slant[a] - slant[b])
 
 
 def surface(grad):
@@ -209,7 +200,7 @@
     return [x * p, y * q, z * r, x * q, x * r, y * r]
 
 
-def step_one(label, dens, vel, grad, store_post, store_red):
+def step_one(label, dens, vel, grad):
     scale = LEFT * W2
     mix = label * (1.0 - label) * dens
     gmag, inv = surface(grad)
@@ -228,7 +219,7 @@
     tensor = [t + s for t, s in zip(tensor, products([pull * g for g in grad], grad))]
     gm = (0.5 * surface_amp * scale) * gmag
     h = (recolouring_strength * scale) * mix * inv
-    collide(rest - gm, 12.0 * (rest + gm), tensor, flow, [h * g for g in grad], label, None, store_post, store_red)
+    return collide(rest - gm, 12.0 * (rest + gm), tensor, flow, [h * g for g in grad], label, None)
 
 
 def moment(pops, a):
@@ -240,7 +231,7 @@
     return total
 
 
-def step_two(rho, rinv, share, tail, grad, store_post, store_red):
+def step_two(rho, rinv, share, tail, grad):
     mix = share * (1.0 - share) * rho
     gmag, inv = surface(grad)
     scaled = [moment(tail, a) for a in range(3)]
@@ -252,15 +243,15 @@
     tensor = [t + s for t, s in zip(tensor, products([pull * g for g in grad], grad))]
     gm = (0.5 * surface_amp * W2) * gmag
     h = (recolouring_strength * W2) * mix * inv
-    collide(rest - gm, 12.0 * (rest + gm), tensor, flow, [h * g for g in grad], share, tail, store_post, store_red)
-
-
-def streamed_parts(load, weight=None):
+    return collide(rest - gm, 12.0 * (rest + gm), tensor, flow, [h * g for g in grad], share, tail)
+
+
+def streamed_parts(values, weight=None):
     parts = {0: [], 1: [], -1: []}
     for i, c in enumerate(VELOCITIES):
         w = 1 if weight is None else c[weight]
         if w:
-            parts[c[0]].append((load(i), w))
+            parts[c[0]].append((values[i], w))
 
     def tree(terms):
         while len(terms) > 1:
@@ -284,84 +275,102 @@
     return side if parts[0] is None else parts[0] + side
 
 
-def pass_a(refs, j, k):
-    label, raw, post1, red1 = refs["label"], refs["raw"], refs["post1"], refs["red1"]
-    grad = gradient(lambda dy, dz: label[j + 1 + dy, 1 + dz + k : 9 + dz + k, :])
-    tile = lambda at: raw[at, j + 1, 1 + k : 9 + k, :]
-
-    def store_post(i, v):
-        post1[i, j, k : k + 8, :] = v
-
-    def store_red(i, v):
-        red1[i, j, k : k + 8, :] = v
-
-    step_one(label[j + 1, 1 + k : 9 + k, :], tile(0), [tile(1), tile(2), tile(3)], grad, store_post, store_red)
-
-
-def pass_b(refs, j, k):
-    def total(ref):
-        def load(i):
-            _, cy, cz = VELOCITIES[i]
-            return ref[i, j + 1 - cy, 1 - cz + k : 9 - cz + k, :]
-
-        return joined(streamed_parts(load)) * (1.0 / LEFT)
-
-    rho = total(refs["post1"])
+def load_a(refs, j, k):
+    label, raw = refs["label"], refs["raw"]
+    near = {(dy, dz): label[j + 1 + dy, 1 + dz + k : 9 + dz + k, :] for dy in (-1, 0, 1) for dz in (-1, 0, 1)}
+    return near, [raw[at, j + 1, 1 + k : 9 + k, :] for at in range(4)]
+
+
+def pass_a(refs, j, k, loaded):
+    near, (dens, *vel) = loaded
+    for i, post, red in step_one(near[0, 0], dens, vel, gradient(near)):
+        yield refs["post1"].at[i], j, k, post
+        yield refs["red1"].at[i], j, k, red
+
+
+def load_b(refs, j, k):
+    out = []
+    for name in ("post1", "red1"):
+        ref = refs[name]
+        out.append([ref[i, j + 1 - cy, 1 - cz + k : 9 - cz + k, :] for i, (_, cy, cz) in enumerate(VELOCITIES)])
+    return out
+
+
+def pass_b(refs, j, k, loaded):
+    rho, red = [joined(streamed_parts(v)) * (1.0 / LEFT) for v in loaded]
     rinv = 1.0 / rho
-    refs["rho_s"][j, k : k + 8, :] = rho
-    refs["rinv_s"][j, k : k + 8, :] = rinv
-    refs["share_s"][j, k : k + 8, :] = total(refs["red1"]) * rinv
-
-
-def pass_c(refs, j, k):
-    post1, post2, red2, share = refs["post1"], refs["post2"], refs["red2"], refs["share_s"]
-    tail = []
-    for i, (cx, cy, cz) in enumerate(VELOCITIES):
-        tail.append(rolled(post1[i, j + 2 - cy, 2 - cz + k : 10 - cz + k, :], cx))
-    grad = gradient(lambda dy, dz: share[j + 1 + dy, 1 + dz + k : 9 + dz + k, :])
-    tile = lambda ref: ref[j + 1, 1 + k : 9 + k, :]
-
-    def store_post(i, v):
-        post2[i, j, k : k + 8, :] = v
-
-    def store_red(i, v):
-        red2[i, j, k : k + 8, :] = v
-
-    step_two(tile(refs["rho_s"]), tile(refs["rinv_s"]), tile(share), tail, grad, store_post, store_red)
-
-
-def pass_d(refs, j, k, store):
-    def load_of(ref):
-        held = {}
-
-        def load(i):
-            if i not in held:
-                _, cy, cz = VELOCITIES[i]
-                held[i] = ref[i, j + 1 - cy, 1 - cz + k : 9 - cz + k, :]
-            return held[i]
-
-        return load
-
-    load = load_of(refs["post2"])
-    parts = streamed_parts(load)
+    yield refs["rho_s"], j, k, rho
+    yield refs["rinv_s"], j, k, rinv
+    yield refs["share_s"], j, k, red * rinv
+
+
+def load_c(refs, j, k):
+    post1, share = refs["post1"], refs["share_s"]
+    tail = [rolled(post1[i, j + 2 - cy, 2 - cz + k : 10 - cz + k, :], cx) for i, (cx, cy, cz) in enumerate(VELOCITIES)]
+    near = {(dy, dz): share[j + 1 + dy, 1 + dz + k : 9 + dz + k, :] for dy in (-1, 0, 1) for dz in (-1, 0, 1)}
+    return tail, near, [refs[name][j + 1, 1 + k : 9 + k, :] for name in ("rho_s", "rinv_s")]
+
+
+def pass_c(refs, j, k, loaded):
+    tail, near, (rho, rinv) = loaded
+    for i, post, red in step_two(rho, rinv, near[0, 0], tail, gradient(near)):
+        yield refs["post2"].at[i], j, k, post
+        yield refs["red2"].at[i], j, k, red
+
+
+def load_d(refs, j, k):
+    out = []
+    for name in ("post2", "red2"):
+        ref = refs[name]
+        out.append([ref[i, j + 1 - cy, 1 - cz + k : 9 - cz + k, :] for i, (_, cy, cz) in enumerate(VELOCITIES)])
+    return out
+
+
+def pass_d(refs, j, k, loaded):
+    post, red = loaded
+    parts = streamed_parts(post)
     up, down = rolled(parts[1], 1), rolled(parts[-1], -1)
     rho = parts[0] + (up + down)
-    red = joined(streamed_parts(load_of(refs["red2"])))
-    store(j, k, [red, rho - red, up - down, joined(streamed_parts(load, 1)), joined(streamed_parts(load, 2))])
-
-
-def sweep(work, refs, rows, chunks, unroll):
+    red = joined(streamed_parts(red))
+    for at, v in enumerate([red, rho - red, up - down, joined(streamed_parts(post, 1)), joined(streamed_parts(post, 2))]):
+        yield refs["edge"].at[at], j, k, v
+
+
+PASSES = dict(a=(load_a, pass_a, 3, False), b=(load_b, pass_b, 1, True), c=(load_c, pass_c, 1, False), d=(load_d, pass_d, 1, True))
+
+
+def sweep(name, refs, rows, chunks, per, shift=0):
+    load, work, group, defer = PASSES[name]
     count = rows[0][1] - rows[0][0]
 
+    def put(ref, j, k, value):
+        ref[j - shift, k : k + 8, :] = value
+
+    def trip(t, n):
+        tiles = [(start + t + r, k) for r in range(n) for start, _ in rows for k in chunks]
+        waiting = []
+        for at in range(0, len(tiles), group):
+            some = tiles[at : at + group]
+            held = [load(refs, j, k) for j, k in some]
+            for (j, k), loaded in zip(some, held):
+                for item in work(refs, j, k, loaded):
+                    if defer:
+                        waiting.append(item)
+                    else:
+                        put(*item)
+        for item in waiting:
+            put(*item)
+
     def body(t, carry):
-        for start, _ in rows:
-            for k in chunks:
-                work(refs, start + t, k)
+        trip(t * per, per)
         return carry
 
-    lax.fori_loop(0, count, body, 0, unroll=unroll)
-
-
+    lax.fori_loop(0, count // per, body, 0)
+    if count % per:
+        trip(count - count % per, count % per)
+
+
+PER = 4
 STATE = dict(
     label=(24, 32, 128),
     raw=(4, 24, 32, 128),
@@ -409,17 +418,14 @@
     either(is_odd("gz"), assemble)
     either(is_odd("gy"), beside)
 
-    def store(j, k, values):
-        for at, v in enumerate(values):
-            done[at, j - 4, k : k + 8, :] = v
-
-    sweep(pass_a, refs, [(4, 18)], A_Z, 2)
-    sweep(pass_a, refs, [(0, 4), (18, 22)], A_Z[1:2], 2)
-    sweep(pass_b, refs, [(4, 16)], B_Z, 2)
-    sweep(pass_b, refs, [(0, 4), (16, 20)], B_Z[1:2], 2)
-    sweep(pass_c, refs, [(4, 14)], C_Z, 2)
-    sweep(pass_c, refs, [(0, 4), (14, 18)], C_Z[1:2], 2)
-    sweep(lambda r, j, k: pass_d(r, j, k, store), refs, [(4, 12)], D_Z, 2)
+    refs["edge"] = done
+    sweep("a", refs, [(4, 18)], A_Z, PER)
+    sweep("a", refs, [(0, 4), (18, 22)], A_Z[1:2], PER)
+    sweep("b", refs, [(4, 16)], B_Z, PER)
+    sweep("b", refs, [(0, 4), (16, 20)], B_Z[1:2], PER)
+    sweep("c", refs, [(4, 14)], C_Z, PER)
+    sweep("c", refs, [(0, 4), (14, 18)], C_Z[1:2], PER)
+    sweep("d", refs, [(4, 12)], D_Z, PER, shift=4)
 
 
 def outer(y_ev, y_od, done, *rest):
@@ -446,23 +452,12 @@
 
     either(is_odd("gy"), corners)
 
-    def store_low(j, k, values):
-        for at, v in enumerate(values):
-            edge[at, j, k : k + 8, :] = v
-
-    def store_high(j, k, values):
-        for at, v in enumerate(values):
-            edge[at, j - 8, k : k + 8, :] = v
-
-    sweep(pass_a, refs, [(0, 4), (18, 22)], A_Z[::2], 2)
-    sweep(pass_b, refs, [(0, 4), (16, 20)], B_Z[::2], 2)
-    sweep(pass_c, refs, [(0, 4), (14, 18)], C_Z[::2], 2)
-
-    def last(r, t, k):
-        pass_d(r, t, k, store_low)
-        pass_d(r, t + 12, k, store_high)
-
-    sweep(last, refs, [(0, 4)], D_Z, 2)
+    refs["edge"] = edge
+    sweep("a", refs, [(0, 4), (18, 22)], A_Z[::2], PER)
+    sweep("b", refs, [(0, 4), (16, 20)], B_Z[::2], PER)
+    sweep("c", refs, [(0, 4), (14, 18)], C_Z[::2], PER)
+    sweep("d", refs, [(0, 4)], D_Z, PER)
+    sweep("d", refs, [(12, 16)], D_Z, PER, shift=8)
     second = send(edge, 0, (0, 4), 1) + send(edge, 4, (12, 4), 2)
     for c in second:
         c.start()
@@ -484,6 +479,7 @@
 
 
 def shards(phase, density, velocity):
+    phase, density, velocity = [pltpu.with_memory_space_constraint(v, pltpu.HBM) for v in (phase, density, velocity)]
     in_vmem = pl.BlockSpec(memory_space=pltpu.VMEM)
     in_hbm = pl.BlockSpec(memory_space=pltpu.HBM)
     state = [f32(*s) for s in STATE.values()]

time: 28.8 us -> 24.9 us (0.86)
  local copies, waits for them, and re-layouts: 2.8 us -> 0 us
  Pallas kernels: 9.09 us -> 8.02 us
    unnamed x6 -> x0, local copies, waits for them, and re-layouts: 2.8 us -> none
    pallas_call x1, Pallas kernels: 5.63 us -> 4.43 us  [shards(): pl.pallas_call(inner, out_shape=tuple(state) + (f32(5, 8, 16, 128),), com...]
    pallas_call x1, Pallas kernels: 0.65 us -> 1.2 us  [shards(): pl.pallas_call(pack_own, out_shape=(jax.ShapeDtypeStruct((16, 16, 128), j...]
    pallas_call x1, Pallas kernels: 2.79 us -> 2.37 us  [shards(): pl.pallas_call(outer, out_shape=tuple(state) + (f32(16, 16, 128), f32(16,...]
  transfers between devices with their start and end apart: 6 -> 6, of which waited for: 2 -> 2; matrix products, arithmetic and copies ran while one was open for 0% -> 0% of each run, Pallas kernels for 20% -> 18%
where the time goes in v3:
time: 24.9 us; the launch traced here: 24.8 us
  starting transfers between devices  12 us (48%)
  Pallas kernels  8.02 us (32%)
  waiting for transfers between devices  4.09 us (16%)
  between operations  0.67 us (3%)
    ppermute x6, starting transfers between devices, swap(): return lax.ppermute(value, axis, pairs)  12 us
    pallas_call x1, Pallas kernels, shards(): pl.pallas_call(inner, out_shape=tuple(state) + (f32(5, 8, 16, 128),), com...  4.43 us
    ppermute x6, waiting for transfers between devices, swap(): return lax.ppermute(value, axis, pairs)  4.09 us
    pallas_call x1, Pallas kernels, shards(): pl.pallas_call(outer, out_shape=tuple(state) + (f32(16, 16, 128), f32(16,...  2.37 us
    pallas_call x1, Pallas kernels, shards(): pl.pallas_call(pack_own, out_shape=(jax.ShapeDtypeStruct((16, 16, 128), j...  1.2 us
  transfers between devices with their start and end apart: 6, of which 2 were waited for; matrix products, arithmetic and copies ran while one was open for 0% of the time, Pallas kernels for 18%

profile of v3, /device:TPU:27, one launch (start us, length us, event | category | flops | bytes accessed | tf_op | source)
XLA Modules:
  0.0 24.8 jit_solution(11072879102643027369)
XLA Ops:
  0.6 1.2 %shard_map.58 = (s32[16,16,128]{2,1,0:T(8,128)S(1)}, f32[16,16,128]{2,1,0:T(8,128)S(1)}, f32[3,16,16,128]{3,2,1,0:T(8,128)S(1)}, f32[16,16,128]{2,1,0:T(8,128)S(...) custom-call(s32[16,16,128]{2,1,0:T(8,128)} %phase_in.1, ...), custom_call_target="tpu_custom_call" | custom-call | tf_op jit(solution)/shard_map/pallas_call | solution.py:486
  1.8 1.9 %collective-permute-start = (f32[16,16,128]{2,1,0:T(8,128)S(1)}, f32[16,16,128]{2,1,0:T(8,128)S(1)}, u32[]{:S(2)}, u32[]{:S(2)}) collective-permute-start(f32[16,16,128]{2,1,0:T(8,128)S(1)} %get-tuple-element.25), channel_id=1, source_target_pairs={{0,1},{1,0},{2,3},{3,2},{4,5},{5,4},{6,7},{7,6},{8,9},{9,8},{10,11... | collective-permute-start | bytes 393224 | tf_op jit(solution)/shard_map/ppermute | solution.py:478
  3.8 6.4 %collective-permute-start.1 = (f32[16,16,128]{2,1,0:T(8,128)S(1)}, f32[16,16,128]{2,1,0:T(8,128)S(1)}, u32[]{:S(2)}, u32[]{:S(2)}) collective-permute-start(f32[16,16,128]{2,1,0:T(8,128)S(1)} %get-tuple-element.26), channel_id=1, source_target_pairs={{1,2},{2,1},{3,4},{4,3},{5,6},{6,5},{7,8},{8,7},{9,10},{10,9},{11,... | collective-permute-start | bytes 393224 | tf_op jit(solution)/shard_map/ppermute | solution.py:478
  10.2 1.2 %collective-permute-start.4 = (f32[16,16,128]{2,1,0:T(8,128)S(1)}, f32[16,16,128]{2,1,0:T(8,128)S(1)}, u32[]{:S(2)}, u32[]{:S(2)}) collective-permute-start(f32[16,16,128]{2,1,0:T(8,128)S(1)} %get-tuple-element.32), channel_id=1, source_target_pairs={{0,16},{16,0},{32,48},{48,32},{64,80},{80,64},{96,112},{112,96},{1... | collective-permute-start | bytes 393224 | tf_op jit(solution)/shard_map/ppermute | solution.py:478
  11.4 0.0 collective-permute-start.5
  11.4 0.0 collective-permute-done.from_ev.z_ev
  11.4 1.7 %collective-permute-done.1.from_od.z_od = f32[16,16,128]{2,1,0:T(8,128)S(1)} collective-permute-done((f32[16,16,128]{2,1,0:T(8,128)S(1)}, f32[16,16,128]{2,1,0:T(8,128)S(1)}, u32[]{:S(2)}, u32[]{:S(2)}) %collective-permute-start.1) | collective-permute-done | bytes 131104 | tf_op jit(solution)/shard_map/ppermute | solution.py:478
  13.1 1.7 %collective-permute-start.2 = (f32[16,8,128]{2,1,0:T(8,128)S(1)}, f32[16,8,128]{2,1,0:T(8,128)S(1)}, u32[]{:S(2)}, u32[]{:S(2)}) collective-permute-start(f32[16,8,128]{2,1,0:T(8,128)S(1)} %get-tuple-element.27), channel_id=1, source_target_pairs={{0,16},{16,0},{32,48},{48,32},{64,80},{80,64},{96,112},{112,96},{1... | collective-permute-start | bytes 196616 | tf_op jit(solution)/shard_map/ppermute | solution.py:478
  14.9 0.6 %collective-permute-start.3 = (f32[16,8,128]{2,1,0:T(8,128)S(1)}, f32[16,8,128]{2,1,0:T(8,128)S(1)}, u32[]{:S(2)}, u32[]{:S(2)}) collective-permute-start(f32[16,8,128]{2,1,0:T(8,128)S(1)} %get-tuple-element.28), channel_id=1, source_target_pairs={{16,32},{32,16},{48,64},{64,48},{80,96},{96,80},{112,128},{128,112... | collective-permute-start | bytes 196616 | tf_op jit(solution)/shard_map/ppermute | solution.py:478
  15.5 0.0 collective-permute-done.4.y_ev
  15.5 2.4 %collective-permute-done.5.y_od = f32[16,16,128]{2,1,0:T(8,128)S(1)} collective-permute-done((f32[16,16,128]{2,1,0:T(8,128)S(1)}, f32[16,16,128]{2,1,0:T(8,128)S(1)}, u32[]{:S(2)}, u32[]{:S(2)}) %collective-permute-start.5) | collective-permute-done | bytes 131104 | tf_op jit(solution)/shard_map/ppermute | solution.py:478
  17.9 4.4 %shard_map.60 = (f32[24,32,128]{2,1,0:T(8,128)S(1)}, f32[4,24,32,128]{3,2,1,0:T(8,128)S(1)}, f32[19,22,32,128]{3,2,1,0:T(8,128)S(1)}, f32[19,22,32,128]{3,2,1,0:...) custom-call(s32[16,16,128]{2,1,0:T(8,128)S(1)} %get-tuple-element.29, ...), custom_call_target="tpu_custom_call" | custom-call | flops 40000000 | bytes 20000000 | tf_op jit(solution)/shard_map/pallas_call | solution.py:501
  22.4 0.0 collective-permute-done.2.y_ev
  22.4 0.0 collective-permute-done.3.y_od
  22.4 2.4 %shard_map.61 = (f32[24,32,128]{2,1,0:T(8,128)S(1)}, f32[4,24,32,128]{3,2,1,0:T(8,128)S(1)}, f32[19,22,32,128]{3,2,1,0:T(8,128)S(1)}, f32[19,22,32,128]{3,2,1,0:...) custom-call(f32[16,8,128]{2,1,0:T(8,128)S(1)} %collective-permute-do, ...), custom_call_target="tpu_custom_call", output_to_operand_aliasing={{0}: (3, {}), {1}: (4, {}), {2}: (5, {}), {3}: (6, {}), {4}... | custom-call | tf_op jit(solution)/shard_map/pallas_call | solution.py:508
  (1 shorter events, 0.0 us)
Async XLA Ops:
  1.8 9.6 %collective-permute-start = (f32[16,16,128]{2,1,0:T(8,128)S(1)}, f32[16,16,128]{2,1,0:T(8,128)S(1)}, u32[]{:S(2)}, u32[]{:S(2)}) collective-permute-start(f32[16,16,128]{2,1,0:T(8,128)S(1)} %get-tuple-element.25), channel_id=1, source_target_pairs={{0,1},{1,0},{2,3},{3,2},{4,5},{5,4},{6,7},{7,6},{8,9},{9,8},{10,11... | collective-permute-start | bytes 393224 | tf_op jit(solution)/shard_map/ppermute | solution.py:478
  3.8 9.3 %collective-permute-start.1 = (f32[16,16,128]{2,1,0:T(8,128)S(1)}, f32[16,16,128]{2,1,0:T(8,128)S(1)}, u32[]{:S(2)}, u32[]{:S(2)}) collective-permute-start(f32[16,16,128]{2,1,0:T(8,128)S(1)} %get-tuple-element.26), channel_id=1, source_target_pairs={{1,2},{2,1},{3,4},{4,3},{5,6},{6,5},{7,8},{8,7},{9,10},{10,9},{11,... | collective-permute-start | bytes 393224 | tf_op jit(solution)/shard_map/ppermute | solution.py:478
  10.2 5.3 %collective-permute-start.4 = (f32[16,16,128]{2,1,0:T(8,128)S(1)}, f32[16,16,128]{2,1,0:T(8,128)S(1)}, u32[]{:S(2)}, u32[]{:S(2)}) collective-permute-start(f32[16,16,128]{2,1,0:T(8,128)S(1)} %get-tuple-element.32), channel_id=1, source_target_pairs={{0,16},{16,0},{32,48},{48,32},{64,80},{80,64},{96,112},{112,96},{1... | collective-permute-start | bytes 393224 | tf_op jit(solution)/shard_map/ppermute | solution.py:478
  11.4 6.5 %collective-permute-start.5 = (f32[16,16,128]{2,1,0:T(8,128)S(1)}, f32[16,16,128]{2,1,0:T(8,128)S(1)}, u32[]{:S(2)}, u32[]{:S(2)}) collective-permute-start(f32[16,16,128]{2,1,0:T(8,128)S(1)} %get-tuple-element.33), channel_id=1, source_target_pairs={{16,32},{32,16},{48,64},{64,48},{80,96},{96,80},{112,128},{128,112... | collective-permute-start | bytes 393224 | tf_op jit(solution)/shard_map/ppermute | solution.py:478
  13.1 9.2 %collective-permute-start.2 = (f32[16,8,128]{2,1,0:T(8,128)S(1)}, f32[16,8,128]{2,1,0:T(8,128)S(1)}, u32[]{:S(2)}, u32[]{:S(2)}) collective-permute-start(f32[16,8,128]{2,1,0:T(8,128)S(1)} %get-tuple-element.27), channel_id=1, source_target_pairs={{0,16},{16,0},{32,48},{48,32},{64,80},{80,64},{96,112},{112,96},{1... | collective-permute-start | bytes 196616 | tf_op jit(solution)/shard_map/ppermute | solution.py:478
  14.9 7.5 %collective-permute-start.3 = (f32[16,8,128]{2,1,0:T(8,128)S(1)}, f32[16,8,128]{2,1,0:T(8,128)S(1)}, u32[]{:S(2)}, u32[]{:S(2)}) collective-permute-start(f32[16,8,128]{2,1,0:T(8,128)S(1)} %get-tuple-element.28), channel_id=1, source_target_pairs={{16,32},{32,16},{48,64},{64,48},{80,96},{96,80},{112,128},{128,112... | collective-permute-start | bytes 196616 | tf_op jit(solution)/shard_map/ppermute | solution.py:478

commit v4 on v3

--- a/solution.py
+++ b/solution.py
@@ -1,3 +1,4 @@
+import functools
 import math
 
 import jax
@@ -88,7 +89,7 @@
         work(False)
 
 
-def pack_own(phase_in, density_in, velocity_in, phase, density, velocity, z_ev, z_od, y_ev, y_od, sems):
+def pack_own(phase_in, density_in, velocity_in, phase, density, velocity, z_ev, z_od, y_od, y_ev, sems):
     copies = [
         pltpu.make_async_copy(velocity_in, velocity, sems.at[0]),
         pltpu.make_async_copy(density_in, density, sems.at[1]),
@@ -112,19 +113,50 @@
     either(is_odd("gy"), along_y)
 
 
-def pack_corners(from_ev, from_od, msg_ev, msg_od):
+def row_index():
+    return lax.broadcasted_iota(jnp.int32, (8, 128), 0)
+
+
+def take_rows(tile, index):
+    return jnp.take_along_axis(tile, index, axis=0)
+
+
+def fold(low, low_at, high, high_at):
+    row = row_index()
+    q = lax.shift_right_logical(row, 1)
+    odd = lax.rem(row, 2) == 1
+    return jnp.where(odd, take_rows(high, high_at(q)), take_rows(low, low_at(q)))
+
+
+def mirror(at, tile):
+    return jnp.where(lax.rem(row_index(), 2) == 1, -tile, tile) if at == 3 else tile
+
+
+def fold_halo(at, low, high, y):
+    start, off = (8, 4) if at == 4 else (8, 1) if at == 3 else (3 * at, 0)
+    n = depth(at)
+    low, high = low[y, start : start + 8, :], high[y, start : start + 8, :]
+    return mirror(at, fold(low, lambda q: off + jnp.maximum(q - (4 - n), 0), high, lambda q: off + jnp.minimum(3 - q, n - 1)))
+
+
+def fold_own(at, plane):
+    low, high = plane[0:8, :], plane[8:16, :]
+    tiles = [
+        fold(low, lambda q: q, high, lambda q: 7 - q),
+        fold(low, lambda q: 4 + q, high, lambda q: 3 - q),
+        fold(high, lambda q: q, low, lambda q: 7 - q),
+    ]
+    return [mirror(at, t) for t in tiles]
+
+
+def pack_corners(from_ev, from_od, after, msg_od, msg_ev):
     odd_y = is_odd("gy")
 
     def fill(msg, low, z_low, z_high):
         for at in range(5):
             n = depth(at)
             for k in range(n):
-                y = k if low else 16 - n + k
-                row = 3 * at + k
-                if n == 3:
-                    msg[row] = jnp.zeros((8, 128), jnp.float32)
-                msg[row, 4 - n : 4, :] = z_low[y, 3 * at : 3 * at + n, :]
-                msg[row, 4 : 4 + n, :] = z_high[y, 3 * at : 3 * at + n, :]
+                msg[3 * at + k] = fold_halo(at, z_low, z_high, k if low else 16 - n + k)
 
     def along_z(odd_z):
         z_low, z_high = (from_ev, from_od) if odd_z else (from_od, from_ev)
@@ -275,10 +307,12 @@
     return side if parts[0] is None else parts[0] + side
 
 
+def around(ref, j, k):
+    return {(dy, dz): ref[j + dy, 2 + 2 * dz + k : 10 + 2 * dz + k, :] for dy in (-1, 0, 1) for dz in (-1, 0, 1)}
+
+
 def load_a(refs, j, k):
-    label, raw = refs["label"], refs["raw"]
-    near = {(dy, dz): label[j + 1 + dy, 1 + dz + k : 9 + dz + k, :] for dy in (-1, 0, 1) for dz in (-1, 0, 1)}
-    return near, [raw[at, j + 1, 1 + k : 9 + k, :] for at in range(4)]
+    return around(refs["label"], j + 1, k), [refs["raw"][at, j + 1, 2 + k : 10 + k, :] for at in range(4)]
 
 
 def pass_a(refs, j, k, loaded):
@@ -288,12 +322,12 @@
         yield refs["red1"].at[i], j, k, red
 
 
+def incoming(ref, j, k):
+    return [ref[i, j - cy, 2 - 2 * cz + k : 10 - 2 * cz + k, :] for i, (_, cy, cz) in enumerate(VELOCITIES)]
+
+
 def load_b(refs, j, k):
-    out = []
-    for name in ("post1", "red1"):
-        ref = refs[name]
-        out.append([ref[i, j + 1 - cy, 1 - cz + k : 9 - cz + k, :] for i, (_, cy, cz) in enumerate(VELOCITIES)])
-    return out
+    return incoming(refs["post1"], j + 1, k), incoming(refs["red1"], j + 1, k)
 
 
 def pass_b(refs, j, k, loaded):
@@ -305,10 +339,8 @@
 
 
 def load_c(refs, j, k):
-    post1, share = refs["post1"], refs["share_s"]
-    tail = [rolled(post1[i, j + 2 - cy, 2 - cz + k : 10 - cz + k, :], cx) for i, (cx, cy, cz) in enumerate(VELOCITIES)]
-    near = {(dy, dz): share[j + 1 + dy, 1 + dz + k : 9 + dz + k, :] for dy in (-1, 0, 1) for dz in (-1, 0, 1)}
-    return tail, near, [refs[name][j + 1, 1 + k : 9 + k, :] for name in ("rho_s", "rinv_s")]
+    tail = [rolled(v, c[0]) for v, c in zip(incoming(refs["post1"], j + 2, k + 2), VELOCITIES)]
+    return tail, around(refs["share_s"], j + 1, k), [refs[name][j + 1, 2 + k : 10 + k, :] for name in ("rho_s", "rinv_s")]
 
 
 def pass_c(refs, j, k, loaded):
@@ -319,11 +351,7 @@
 
 
 def load_d(refs, j, k):
-    out = []
-    for name in ("post2", "red2"):
-        ref = refs[name]
-        out.append([ref[i, j + 1 - cy, 1 - cz + k : 9 - cz + k, :] for i, (_, cy, cz) in enumerate(VELOCITIES)])
-    return out
+    return incoming(refs["post2"], j + 1, k), incoming(refs["red2"], j + 1, k)
 
 
 def pass_d(refs, j, k, loaded):
@@ -332,48 +360,59 @@
     up, down = rolled(parts[1], 1), rolled(parts[-1], -1)
     rho = parts[0] + (up + down)
     red = joined(streamed_parts(red))
-    for at, v in enumerate([red, rho - red, up - down, joined(streamed_parts(post, 1)), joined(streamed_parts(post, 2))]):
-        yield refs["edge"].at[at], j, k, v
-
-
-PASSES = dict(a=(load_a, pass_a, 3, False), b=(load_b, pass_b, 1, True), c=(load_c, pass_c, 1, False), d=(load_d, pass_d, 1, True))
-
-
-def sweep(name, refs, rows, chunks, per, shift=0):
-    load, work, group, defer = PASSES[name]
+    row = row_index()
+    mom_z = joined(streamed_parts(post, 2))
+    mom_z = jnp.where(lax.rem(row, 2) == 1, -mom_z, mom_z)
+    if k == 0:
+        index, at_first, at_last = jnp.where(row < 4, 2 * row, 15 - 2 * row), 0, 12
+    else:
+        index, at_first, at_last = jnp.where(row < 4, 7 - 2 * row, 2 * row - 8), 8, 4
+    for at, v in enumerate([red, rho - red, up - down, joined(streamed_parts(post, 1)), mom_z]):
+        v = take_rows(v, index)
+        yield refs["edge"].at[at], j, at_first, v[0:4]
+        yield refs["edge"].at[at], j, at_last, v[4:8]
+
+
+PASSES = dict(a=(load_a, pass_a, False), b=(load_b, pass_b, True), c=(load_c, pass_c, False), d=(load_d, pass_d, True))
+
+
+def sweep(name, refs, rows, tiles, per):
+    load, work, defer = PASSES[name]
     count = rows[0][1] - rows[0][0]
 
     def put(ref, j, k, value):
-        ref[j - shift, k : k + 8, :] = value
+        ref[j, k : k + value.shape[0], :] = value
 
     def trip(t, n):
-        tiles = [(start + t + r, k) for r in range(n) for start, _ in rows for k in chunks]
         waiting = []
-        for at in range(0, len(tiles), group):
-            some = tiles[at : at + group]
-            held = [load(refs, j, k) for j, k in some]
-            for (j, k), loaded in zip(some, held):
-                for item in work(refs, j, k, loaded):
-                    if defer:
-                        waiting.append(item)
-                    else:
-                        put(*item)
+        for r in range(n):
+            for start, _ in rows:
+                for k in tiles:
+                    j = start + t + r
+                    for item in work(refs, j, k, load(refs, j, k)):
+                        if defer:
+                            waiting.append(item)
+                        else:
+                            put(*item)
         for item in waiting:
             put(*item)
 
-    def body(t, carry):
-        trip(t * per, per)
-        return carry
-
-    lax.fori_loop(0, count // per, body, 0)
+    if count // per > 1:
+
+        def body(t, carry):
+            trip(t * per, per)
+            return carry
+
+        lax.fori_loop(0, count // per, body, 0)
+    else:
+        trip(0, per)
     if count % per:
         trip(count - count % per, count % per)
 
 
-PER = 4
 STATE = dict(
-    label=(24, 32, 128),
-    raw=(4, 24, 32, 128),
+    label=(24, 40, 128),
+    raw=(4, 24, 40, 128),
     post1=(19, 22, 32, 128),
     red1=(19, 22, 32, 128),
     rho_s=(20, 32, 128),
@@ -381,84 +420,111 @@
     share_s=(20, 32, 128),
     post2=(19, 18, 24, 128),
     red2=(19, 18, 24, 128),
+    edge=(5, 16, 16, 128),
 )
 NAMES = list(STATE)
-A_Z, B_Z, C_Z, D_Z = (0, 8, 16), (0, 8, 14), (0, 8, 12), (0, 8)
 
 
 def frame_of(refs, at):
     return refs["label"] if at == 4 else refs["raw"].at[at]
 
 
-def inner(phase, density, velocity, z_ev, z_od, y_ev, y_od, *rest):
-    refs = dict(zip(NAMES, rest))
-    done = rest[len(NAMES)]
-
-    def assemble(odd):
-        low, high = (z_ev, z_od) if odd else (z_od, z_ev)
-
+def lay(refs, at, row, plane):
+    for t, tile in enumerate(fold_own(at, plane)):
+        frame_of(refs, at)[row, 8 + 8 * t : 16 + 8 * t, :] = tile
+
+
+def middle(when, part, held, phase, density, velocity, *rest):
+    refs = dict(zip(NAMES, rest[held + 1 :]))
+
+    def early():
         def body(y, carry):
             for at in range(5):
-                ref, n = frame_of(refs, at), depth(at)
-                ref[y + 4, 4:20, :] = own_plane(at, y, phase, density, velocity)
-                ref[y + 4, 4 - n : 4, :] = low[y, 3 * at : 3 * at + n, :]
-                ref[y + 4, 20 : 20 + n, :] = high[y, 3 * at : 3 * at + n, :]
+                lay(refs, at, y + 4, own_plane(at, y, phase, density, velocity))
             return carry
 
         lax.fori_loop(0, 16, body, 0, unroll=2)
-
-    def beside(odd):
+        sweep("a", refs, [(4, 18)], (8, 16, 24), 4)
+
+    def late():
+        sweep("b", refs, [(4, 16)], (8, 16), 6)
+        sweep("c", refs, [(4, 14)], (8, 16), 5)
+        sweep("d", refs, [(4, 12)], (8,), 8)
+
+    pl.when(when())(early)
+    if part:
+        late()
+
+
+def first_z():
+    return lax.axis_index("gz") == 0
+
+
+def later_z():
+    return lax.axis_index("gz") != 0
+
+
+def sides(z_ev, z_od, y_od, y_ev, *rest):
+    refs = dict(zip(NAMES, rest[len(NAMES) :]))
+
+    def assemble_z(odd):
+        low, high = (z_ev, z_od) if odd else (z_od, z_ev)
+
+        def body(y, carry):
+            for at in range(5):
+                frame_of(refs, at)[y + 4, 0:8, :] = fold_halo(at, low, high, y)
+            return carry
+
+        lax.fori_loop(0, 16, body, 0, unroll=4)
+
+    def assemble_y(odd):
         low, high = (y_ev, y_od) if odd else (y_od, y_ev)
         for at in range(5):
-            ref, n = frame_of(refs, at), depth(at)
+            n = depth(at)
             for k in range(n):
-                ref[4 - n + k, 4:20, :] = low[3 * at + k]
-                ref[20 + k, 4:20, :] = high[3 * at + k]
-
-    either(is_odd("gz"), assemble)
-    either(is_odd("gy"), beside)
-
-    refs["edge"] = done
-    sweep("a", refs, [(4, 18)], A_Z, PER)
-    sweep("a", refs, [(0, 4), (18, 22)], A_Z[1:2], PER)
-    sweep("b", refs, [(4, 16)], B_Z, PER)
-    sweep("b", refs, [(0, 4), (16, 20)], B_Z[1:2], PER)
-    sweep("c", refs, [(4, 14)], C_Z, PER)
-    sweep("c", refs, [(0, 4), (14, 18)], C_Z[1:2], PER)
-    sweep("d", refs, [(4, 12)], D_Z, PER, shift=4)
-
-
-def outer(y_ev, y_od, done, *rest):
+                lay(refs, at, 4 - n + k, low[3 * at + k])
+                lay(refs, at, 20 + k, high[3 * at + k])
+
+    either(is_odd("gz"), assemble_z)
+    either(is_odd("gy"), assemble_y)
+    sweep("a", refs, [(0, 4), (18, 22)], (8, 16, 24), 2)
+    sweep("a", refs, [(4, 18)], (0,), 7)
+    sweep("b", refs, [(0, 4), (16, 20)], (8, 16), 2)
+    sweep("b", refs, [(4, 16)], (0,), 12)
+    sweep("c", refs, [(0, 4), (14, 18)], (8, 16), 2)
+    sweep("c", refs, [(4, 14)], (0,), 10)
+    sweep("d", refs, [(0, 4), (12, 16)], (8,), 4)
+    sweep("d", refs, [(4, 12)], (0,), 8)
+
+
+def corners(y_od, y_ev, *rest):
     n = len(NAMES)
     refs = dict(zip(NAMES, rest[n : 2 * n]))
-    out_red, out_blue, out_mom, edge, sems = rest[2 * n :]
-
-    def send(src, rows, at_rows, sem):
+    out_red, out_blue, out_mom, sems = rest[2 * n :]
+
+    def send(start, count, sem):
         outs = [out_red, out_blue, out_mom.at[0], out_mom.at[1], out_mom.at[2]]
-        return [pltpu.make_async_copy(src.at[f, pl.ds(rows, at_rows[1])], outs[f].at[pl.ds(at_rows[0], at_rows[1])], sems.at[sem, f]) for f in range(5)]
-
-    first = send(done, 0, (4, 8), 0)
+        rows = pl.ds(start, count)
+        return [pltpu.make_async_copy(refs["edge"].at[f, rows], outs[f].at[rows], sems.at[sem, f]) for f in range(5)]
+
+    first = send(4, 8, 0)
     for c in first:
         c.start()
 
-    def corners(odd):
+    def assemble(odd):
         low, high = (y_ev, y_od) if odd else (y_od, y_ev)
         for at in range(5):
-            ref, d = frame_of(refs, at), depth(at)
+            d = depth(at)
             for k in range(d):
-                for row, msg in ((4 - d + k, low), (20 + k, high)):
-                    ref[row, 4 - d : 4, :] = msg[3 * at + k, 4 - d : 4, :]
-                    ref[row, 20 : 20 + d, :] = msg[3 * at + k, 4 : 4 + d, :]
-
-    either(is_odd("gy"), corners)
-
-    refs["edge"] = edge
-    sweep("a", refs, [(0, 4), (18, 22)], A_Z[::2], PER)
-    sweep("b", refs, [(0, 4), (16, 20)], B_Z[::2], PER)
-    sweep("c", refs, [(0, 4), (14, 18)], C_Z[::2], PER)
-    sweep("d", refs, [(0, 4)], D_Z, PER)
-    sweep("d", refs, [(12, 16)], D_Z, PER, shift=8)
-    second = send(edge, 0, (0, 4), 1) + send(edge, 4, (12, 4), 2)
+                frame_of(refs, at)[4 - d + k, 0:8, :] = low[3 * at + k]
+                frame_of(refs, at)[20 + k, 0:8, :] = high[3 * at + k]
+
+    either(is_odd("gy"), assemble)
+    sweep("a", refs, [(0, 4), (18, 22)], (0,), 4)
+    sweep("b", refs, [(0, 4), (16, 20)], (0,), 4)
+    sweep("c", refs, [(0, 4), (14, 18)], (0,), 4)
+    sweep("d", refs, [(0, 4), (12, 16)], (0,), 4)
+    second = send(0, 4, 1) + send(12, 4, 2)
     for c in second:
         c.start()
     for c in first + second:
@@ -483,7 +549,7 @@
     in_vmem = pl.BlockSpec(memory_space=pltpu.VMEM)
     in_hbm = pl.BlockSpec(memory_space=pltpu.HBM)
     state = [f32(*s) for s in STATE.values()]
-    phase, density, velocity, z_ev, z_od, y_ev, y_od = pl.pallas_call(
+    phase, density, velocity, z_ev, z_od, y_od, y_ev = pl.pallas_call(
         pack_own,
         out_shape=(jax.ShapeDtypeStruct((16, 16, 128), jnp.int32), f32(16, 16, 128), f32(3, 16, 16, 128)) + (f32(16, 16, 128),) * 4,
         in_specs=[in_hbm] * 3,
@@ -491,29 +557,48 @@
         scratch_shapes=[pltpu.SemaphoreType.DMA((3,))],
         compiler_params=vmem(8),
     )(phase, density, velocity)
+    n = len(NAMES)
+
+    def do_middle(when, held, token):
+        aliases = {3 + i: i for i in range(len(held) + 1)} if held else {3: n}
+        *made, token = pl.pallas_call(
+            functools.partial(middle, when, bool(held), len(held)),
+            out_shape=tuple(state) + (jax.ShapeDtypeStruct(token.shape, token.dtype),),
+            in_specs=[in_vmem] * (4 + len(held)),
+            out_specs=(in_vmem,) * (n + 1),
+            input_output_aliases=aliases,
+            compiler_params=vmem(8),
+            cost_estimate=pl.CostEstimate(flops=40_000_000, bytes_accessed=20_000_000, transcendentals=0),
+        )(phase, density, velocity, *held, token)
+        return made, token
+
+    z_ev = swap(z_ev, "gz", 0)
+    held, z_od = do_middle(first_z, [], z_od)
     z_od = swap(z_od, "gz", 1)
-    z_ev = swap(z_ev, "gz", 0)
     y_od = swap(y_od, "gy", 1)
     y_ev = swap(y_ev, "gy", 0)
-    c_ev, c_od = pl.pallas_call(pack_corners, out_shape=(f32(16, 8, 128),) * 2, compiler_params=vmem(4))(z_ev, z_od)
+    held, token = do_middle(later_z, held, jnp.zeros((8, 128), jnp.float32))
+    c_od, c_ev = pl.pallas_call(pack_corners, out_shape=(f32(16, 8, 128),) * 2, compiler_params=vmem(4))(z_ev, z_od, token)
     c_od = swap(c_od, "gy", 1)
     c_ev = swap(c_ev, "gy", 0)
-    made = pl.pallas_call(
-        inner,
-        out_shape=tuple(state) + (f32(5, 8, 16, 128),),
+    held = pl.pallas_call(
+        sides,
+        out_shape=tuple(state),
+        in_specs=[in_vmem] * (4 + n),
+        out_specs=(in_vmem,) * n,
+        input_output_aliases={4 + i: i for i in range(n)},
         compiler_params=vmem(8),
-        cost_estimate=pl.CostEstimate(flops=40_000_000, bytes_accessed=20_000_000, transcendentals=0),
-    )(phase, density, velocity, z_ev, z_od, y_ev, y_od)
-    n = len(NAMES)
+        cost_estimate=pl.CostEstimate(flops=10_000_000, bytes_accessed=5_000_000, transcendentals=0),
+    )(z_ev, z_od, y_od, y_ev, *held)
     return pl.pallas_call(
-        outer,
+        corners,
         out_shape=tuple(state) + (f32(16, 16, 128), f32(16, 16, 128), f32(3, 16, 16, 128)),
-        in_specs=[in_vmem] * (3 + n),
+        in_specs=[in_vmem] * (2 + n),
         out_specs=(in_vmem,) * n + (in_hbm,) * 3,
-        scratch_shapes=[pltpu.VMEM((5, 8, 16, 128), jnp.float32), pltpu.SemaphoreType.DMA((3, 5))],
-        input_output_aliases={3 + i: i for i in range(n)},
+        scratch_shapes=[pltpu.SemaphoreType.DMA((3, 5))],
+        input_output_aliases={2 + i: i for i in range(n)},
         compiler_params=vmem(8),
-    )(c_ev, c_od, made[n], *made[:n])[n:]
+    )(c_od, c_ev, *held)[n:]
 
 
 def solution(mesh):

time: 24.9 us -> 23.7 us (0.952)
  the two profiles are of different devices: /device:TPU:27 before, /device:TPU:1 now
where the time goes in v4:
time: 23.7 us; the launch traced here: 23.6 us
  starting transfers between devices  13.2 us (56%)
  Pallas kernels  9.63 us (41%)
  between operations  0.7 us (3%)
    ppermute x6, starting transfers between devices, swap(): return lax.ppermute(value, axis, pairs)  13.2 us
    pallas_call x1, Pallas kernels, shards(): pl.pallas_call(sides, out_shape=tuple(state), in_specs=[in_vmem] * (4 + n...  3.49 us
    pallas_call x2, Pallas kernels, do_middle(): pl.pallas_call(functools.partial(middle, when, bool(held), len(held)), ou...  3.06 us
    pallas_call x1, Pallas kernels, shards(): pl.pallas_call(corners, out_shape=tuple(state) + (f32(16, 16, 128), f32(1...  1.83 us
    pallas_call x1, Pallas kernels, shards(): pl.pallas_call(pack_own, out_shape=(jax.ShapeDtypeStruct((16, 16, 128), j...  1.2 us
  transfers between devices with their start and end apart: 6, of which 0 were waited for; matrix products, arithmetic and copies ran while one was open for 0% of the time, Pallas kernels for 28%

profile of v4, /device:TPU:1, one launch (start us, length us, event | category | flops | bytes accessed | tf_op | source)
XLA Modules:
  0.0 23.6 jit_solution(16685236088227988080)
XLA Ops:
  0.6 1.2 %shard_map.58 = (s32[16,16,128]{2,1,0:T(8,128)S(1)}, f32[16,16,128]{2,1,0:T(8,128)S(1)}, f32[3,16,16,128]{3,2,1,0:T(8,128)S(1)}, f32[16,16,128]{2,1,0:T(8,128)S(...) custom-call(s32[16,16,128]{2,1,0:T(8,128)} %phase_in.1, ...), custom_call_target="tpu_custom_call" | custom-call | tf_op jit(solution)/shard_map/pallas_call | solution.py:552
  1.8 3.7 %collective-permute-start = (f32[16,16,128]{2,1,0:T(8,128)S(1)}, f32[16,16,128]{2,1,0:T(8,128)S(1)}, u32[]{:S(2)}, u32[]{:S(2)}) collective-permute-start(f32[16,16,128]{2,1,0:T(8,128)S(1)} %get-tuple-element.47), channel_id=1, source_target_pairs={{0,1},{1,0},{2,3},{3,2},{4,5},{5,4},{6,7},{7,6},{8,9},{9,8},{10,11... | collective-permute-start | bytes 393224 | tf_op jit(solution)/shard_map/ppermute | solution.py:544
  5.5 1.8 %shard_map.59 = (f32[24,40,128]{2,1,0:T(8,128)S(1)}, f32[4,24,40,128]{3,2,1,0:T(8,128)S(1)}, f32[19,22,32,128]{3,2,1,0:T(8,128)S(1)}, f32[19,22,32,128]{3,2,1,0:...) custom-call(s32[16,16,128]{2,1,0:T(8,128)S(1)} %get-tuple-element.48, ...), custom_call_target="tpu_custom_call", output_to_operand_aliasing={{10}: (3, {})} | custom-call | flops 40000000 | bytes 20000000 | tf_op jit(solution)/shard_map/pallas_call | solution.py:564
  7.3 3.7 %collective-permute-start.1 = (f32[16,16,128]{2,1,0:T(8,128)S(1)}, f32[16,16,128]{2,1,0:T(8,128)S(1)}, u32[]{:S(2)}, u32[]{:S(2)}) collective-permute-start(f32[16,16,128]{2,1,0:T(8,128)S(1)} %get-tuple-element.52), channel_id=1, source_target_pairs={{1,2},{2,1},{3,4},{4,3},{5,6},{6,5},{7,8},{8,7},{9,10},{10,9},{11,... | collective-permute-start | bytes 393224 | tf_op jit(solution)/shard_map/ppermute | solution.py:544
  11.0 2.4 %collective-permute-start.4 = (f32[16,16,128]{2,1,0:T(8,128)S(1)}, f32[16,16,128]{2,1,0:T(8,128)S(1)}, u32[]{:S(2)}, u32[]{:S(2)}) collective-permute-start(f32[16,16,128]{2,1,0:T(8,128)S(1)} %get-tuple-element.66), channel_id=1, source_target_pairs={{16,32},{32,16},{48,64},{64,48},{80,96},{96,80},{112,128},{128,112... | collective-permute-start | bytes 393224 | tf_op jit(solution)/shard_map/ppermute | solution.py:544
  13.4 1.6 %collective-permute-start.5 = (f32[16,16,128]{2,1,0:T(8,128)S(1)}, f32[16,16,128]{2,1,0:T(8,128)S(1)}, u32[]{:S(2)}, u32[]{:S(2)}) collective-permute-start(f32[16,16,128]{2,1,0:T(8,128)S(1)} %get-tuple-element.67), channel_id=1, source_target_pairs={{0,16},{16,0},{32,48},{48,32},{64,80},{80,64},{96,112},{112,96},{1... | collective-permute-start | bytes 393224 | tf_op jit(solution)/shard_map/ppermute | solution.py:544
  15.1 1.3 %shard_map.60 = (f32[24,40,128]{2,1,0:T(8,128)S(1)}, f32[4,24,40,128]{3,2,1,0:T(8,128)S(1)}, f32[19,22,32,128]{3,2,1,0:T(8,128)S(1)}, f32[19,22,32,128]{3,2,1,0:...) custom-call(s32[16,16,128]{2,1,0:T(8,128)S(1)} %get-tuple-element.48, ...), custom_call_target="tpu_custom_call", output_to_operand_aliasing={{0}: (3, {}), {1}: (4, {}), {2}: (5, {}), {3}: (6, {}), {4}... | custom-call | flops 40000000 | bytes 20000000 | tf_op jit(solution)/shard_map/pallas_call | solution.py:564
  16.3 0.0 collective-permute-done.from_ev.z_ev
  16.4 0.0 collective-permute-done.1.from_od.z_od
  16.4 0.1 shard_map.61
  16.4 1.8 %collective-permute-start.2 = (f32[16,8,128]{2,1,0:T(8,128)S(1)}, f32[16,8,128]{2,1,0:T(8,128)S(1)}, u32[]{:S(2)}, u32[]{:S(2)}) collective-permute-start(f32[16,8,128]{2,1,0:T(8,128)S(1)} %get-tuple-element.64), channel_id=1, source_target_pairs={{16,32},{32,16},{48,64},{64,48},{80,96},{96,80},{112,128},{128,112... | collective-permute-start | bytes 196616 | tf_op jit(solution)/shard_map/ppermute | solution.py:544
  18.2 0.0 collective-permute-start.3
  18.2 0.0 collective-permute-done.4.y_od
  18.2 0.0 collective-permute-done.5.y_ev
  18.2 3.5 %shard_map.62 = (f32[24,40,128]{2,1,0:T(8,128)S(1)}, f32[4,24,40,128]{3,2,1,0:T(8,128)S(1)}, f32[19,22,32,128]{3,2,1,0:T(8,128)S(1)}, f32[19,22,32,128]{3,2,1,0:...) custom-call(f32[16,16,128]{2,1,0:T(8,128)S(1)} %collective-permute-d, ...), custom_call_target="tpu_custom_call", output_to_operand_aliasing={{0}: (4, {}), {1}: (5, {}), {2}: (6, {}), {3}: (7, {}), {4}... | custom-call | flops 10000000 | bytes 5000000 | tf_op jit(solution)/shard_map/pallas_call | solution.py:584
  21.7 0.0 collective-permute-done.2.y_od
  21.7 0.0 collective-permute-done.3.y_ev
  21.8 1.8 %shard_map.63 = (f32[24,40,128]{2,1,0:T(8,128)S(1)}, f32[4,24,40,128]{3,2,1,0:T(8,128)S(1)}, f32[19,22,32,128]{3,2,1,0:T(8,128)S(1)}, f32[19,22,32,128]{3,2,1,0:...) custom-call(f32[16,8,128]{2,1,0:T(8,128)S(1)} %collective-permute-do, ...), custom_call_target="tpu_custom_call", output_to_operand_aliasing={{0}: (2, {}), {1}: (3, {}), {2}: (4, {}), {3}: (5, {}), {4}... | custom-call | tf_op jit(solution)/shard_map/pallas_call | solution.py:593
  (1 shorter events, 0.0 us)
Async XLA Ops:
  1.8 14.5 %collective-permute-start = (f32[16,16,128]{2,1,0:T(8,128)S(1)}, f32[16,16,128]{2,1,0:T(8,128)S(1)}, u32[]{:S(2)}, u32[]{:S(2)}) collective-permute-start(f32[16,16,128]{2,1,0:T(8,128)S(1)} %get-tuple-element.47), channel_id=1, source_target_pairs={{0,1},{1,0},{2,3},{3,2},{4,5},{5,4},{6,7},{7,6},{8,9},{9,8},{10,11... | collective-permute-start | bytes 393224 | tf_op jit(solution)/shard_map/ppermute | solution.py:544
  7.3 9.0 %collective-permute-start.1 = (f32[16,16,128]{2,1,0:T(8,128)S(1)}, f32[16,16,128]{2,1,0:T(8,128)S(1)}, u32[]{:S(2)}, u32[]{:S(2)}) collective-permute-start(f32[16,16,128]{2,1,0:T(8,128)S(1)} %get-tuple-element.52), channel_id=1, source_target_pairs={{1,2},{2,1},{3,4},{4,3},{5,6},{6,5},{7,8},{8,7},{9,10},{10,9},{11,... | collective-permute-start | bytes 393224 | tf_op jit(solution)/shard_map/ppermute | solution.py:544
  11.0 7.2 %collective-permute-start.4 = (f32[16,16,128]{2,1,0:T(8,128)S(1)}, f32[16,16,128]{2,1,0:T(8,128)S(1)}, u32[]{:S(2)}, u32[]{:S(2)}) collective-permute-start(f32[16,16,128]{2,1,0:T(8,128)S(1)} %get-tuple-element.66), channel_id=1, source_target_pairs={{16,32},{32,16},{48,64},{64,48},{80,96},{96,80},{112,128},{128,112... | collective-permute-start | bytes 393224 | tf_op jit(solution)/shard_map/ppermute | solution.py:544
  13.4 4.8 %collective-permute-start.5 = (f32[16,16,128]{2,1,0:T(8,128)S(1)}, f32[16,16,128]{2,1,0:T(8,128)S(1)}, u32[]{:S(2)}, u32[]{:S(2)}) collective-permute-start(f32[16,16,128]{2,1,0:T(8,128)S(1)} %get-tuple-element.67), channel_id=1, source_target_pairs={{0,16},{16,0},{32,48},{48,32},{64,80},{80,64},{96,112},{112,96},{1... | collective-permute-start | bytes 393224 | tf_op jit(solution)/shard_map/ppermute | solution.py:544
  16.4 5.3 %collective-permute-start.2 = (f32[16,8,128]{2,1,0:T(8,128)S(1)}, f32[16,8,128]{2,1,0:T(8,128)S(1)}, u32[]{:S(2)}, u32[]{:S(2)}) collective-permute-start(f32[16,8,128]{2,1,0:T(8,128)S(1)} %get-tuple-element.64), channel_id=1, source_target_pairs={{16,32},{32,16},{48,64},{64,48},{80,96},{96,80},{112,128},{128,112... | collective-permute-start | bytes 196616 | tf_op jit(solution)/shard_map/ppermute | solution.py:544
  18.2 3.5 %collective-permute-start.3 = (f32[16,8,128]{2,1,0:T(8,128)S(1)}, f32[16,8,128]{2,1,0:T(8,128)S(1)}, u32[]{:S(2)}, u32[]{:S(2)}) collective-permute-start(f32[16,8,128]{2,1,0:T(8,128)S(1)} %get-tuple-element.65), channel_id=1, source_target_pairs={{0,16},{16,0},{32,48},{48,32},{64,80},{80,64},{96,112},{112,96},{1... | collective-permute-start | bytes 196616 | tf_op jit(solution)/shard_map/ppermute | solution.py:544

commit v5 on v4

--- a/solution.py
+++ b/solution.py
@@ -434,26 +434,37 @@
         frame_of(refs, at)[row, 8 + 8 * t : 16 + 8 * t, :] = tile
 
 
-def middle(when, part, held, phase, density, velocity, *rest):
-    refs = dict(zip(NAMES, rest[held + 1 :]))
-
-    def early():
+def middle(jobs, held, passed, phase, density, velocity, *rest):
+    refs = dict(zip(NAMES, rest[held + passed :]))
+
+    def lay_own():
         def body(y, carry):
             for at in range(5):
                 lay(refs, at, y + 4, own_plane(at, y, phase, density, velocity))
             return carry
 
         lax.fori_loop(0, 16, body, 0, unroll=2)
-        sweep("a", refs, [(4, 18)], (8, 16, 24), 4)
-
-    def late():
-        sweep("b", refs, [(4, 16)], (8, 16), 6)
-        sweep("c", refs, [(4, 14)], (8, 16), 5)
-        sweep("d", refs, [(4, 12)], (8,), 8)
-
-    pl.when(when())(early)
-    if part:
-        late()
+
+    parts = dict(
+        l=lay_own,
+        a=lambda: sweep("a", refs, [(4, 18)], (8, 16, 24), 14),
+        b=lambda: sweep("b", refs, [(4, 16)], (8, 16), 12),
+        c=lambda: sweep("c", refs, [(4, 14)], (8, 16), 5),
+        d=lambda: sweep("d", refs, [(4, 12)], (8,), 8),
+    )
+    for when, names in jobs:
+
+        def work(names=names):
+            for name in names:
+                parts[name]()
+
+        if when is None:
+            work()
+        else:
+            pl.when(when())(work)
+
+
+FIRST, SECOND, LAST = "la", "bcd", ""
 
 
 def first_z():
@@ -487,11 +498,11 @@
 
     either(is_odd("gz"), assemble_z)
     either(is_odd("gy"), assemble_y)
-    sweep("a", refs, [(0, 4), (18, 22)], (8, 16, 24), 2)
-    sweep("a", refs, [(4, 18)], (0,), 7)
-    sweep("b", refs, [(0, 4), (16, 20)], (8, 16), 2)
+    sweep("a", refs, [(0, 4), (18, 22)], (8, 16, 24), 4)
+    sweep("a", refs, [(4, 18)], (0,), 14)
+    sweep("b", refs, [(0, 4), (16, 20)], (8, 16), 4)
     sweep("b", refs, [(4, 16)], (0,), 12)
-    sweep("c", refs, [(0, 4), (14, 18)], (8, 16), 2)
+    sweep("c", refs, [(0, 4), (14, 18)], (8, 16), 4)
     sweep("c", refs, [(4, 14)], (0,), 10)
     sweep("d", refs, [(0, 4), (12, 16)], (8,), 4)
     sweep("d", refs, [(4, 12)], (0,), 8)
@@ -503,9 +514,9 @@
     out_red, out_blue, out_mom, sems = rest[2 * n :]
 
     def send(start, count, sem):
-        outs = [out_red, out_blue, out_mom.at[0], out_mom.at[1], out_mom.at[2]]
-        rows = pl.ds(start, count)
-        return [pltpu.make_async_copy(refs["edge"].at[f, rows], outs[f].at[rows], sems.at[sem, f]) for f in range(5)]
+        rows, edge = pl.ds(start, count), refs["edge"]
+        pairs = [(edge.at[0, rows], out_red.at[rows]), (edge.at[1, rows], out_blue.at[rows]), (edge.at[2:5, rows], out_mom.at[:, rows])]
+        return [pltpu.make_async_copy(src, dst, sems.at[sem, f]) for f, (src, dst) in enumerate(pairs)]
 
     first = send(4, 8, 0)
     for c in first:
@@ -559,25 +570,31 @@
     )(phase, density, velocity)
     n = len(NAMES)
 
-    def do_middle(when, held, token):
-        aliases = {3 + i: i for i in range(len(held) + 1)} if held else {3: n}
-        *made, token = pl.pallas_call(
-            functools.partial(middle, when, bool(held), len(held)),
-            out_shape=tuple(state) + (jax.ShapeDtypeStruct(token.shape, token.dtype),),
-            in_specs=[in_vmem] * (4 + len(held)),
-            out_specs=(in_vmem,) * (n + 1),
-            input_output_aliases=aliases,
+    def do_middle(jobs, held, *tokens):
+        h, p = len(held), len(tokens)
+        made = pl.pallas_call(
+            functools.partial(middle, jobs, h, p),
+            out_shape=tuple(state) + tuple(jax.ShapeDtypeStruct(t.shape, t.dtype) for t in tokens),
+            in_specs=[in_vmem] * (3 + h + p),
+            out_specs=(in_vmem,) * (n + p),
+            input_output_aliases={3 + i: i + n - h for i in range(h + p)},
             compiler_params=vmem(8),
             cost_estimate=pl.CostEstimate(flops=40_000_000, bytes_accessed=20_000_000, transcendentals=0),
-        )(phase, density, velocity, *held, token)
-        return made, token
-
+        )(phase, density, velocity, *held, *tokens)
+        return made[:n], *made[n:]
+
+    held = []
+    if FIRST:
+        held, z_ev, z_od = do_middle([(first_z, FIRST)], held, z_ev, z_od)
     z_ev = swap(z_ev, "gz", 0)
-    held, z_od = do_middle(first_z, [], z_od)
+    if SECOND:
+        held, z_od = do_middle([(first_z, SECOND)], held, z_od)
     z_od = swap(z_od, "gz", 1)
     y_od = swap(y_od, "gy", 1)
     y_ev = swap(y_ev, "gy", 0)
-    held, token = do_middle(later_z, held, jnp.zeros((8, 128), jnp.float32))
+    early = FIRST + SECOND
+    jobs = [(later_z, early)] + ([(None, LAST)] if LAST else [])
+    held, token = do_middle(jobs, held, jnp.zeros((8, 128), jnp.float32))
     c_od, c_ev = pl.pallas_call(pack_corners, out_shape=(f32(16, 8, 128),) * 2, compiler_params=vmem(4))(z_ev, z_od, token)
     c_od = swap(c_od, "gy", 1)
     c_ev = swap(c_ev, "gy", 0)
@@ -595,7 +612,7 @@
         out_shape=tuple(state) + (f32(16, 16, 128), f32(16, 16, 128), f32(3, 16, 16, 128)),
         in_specs=[in_vmem] * (2 + n),
         out_specs=(in_vmem,) * n + (in_hbm,) * 3,
-        scratch_shapes=[pltpu.SemaphoreType.DMA((3, 5))],
+        scratch_shapes=[pltpu.SemaphoreType.DMA((3, 3))],
         input_output_aliases={2 + i: i for i in range(n)},
         compiler_params=vmem(8),
     )(c_od, c_ev, *held)[n:]

time: 23.7 us -> 22.5 us (0.949)
  Pallas kernels: 9.63 us -> 8.79 us
  starting transfers between devices: 13.2 us -> 12.9 us
    pallas_call x1, Pallas kernels: 3.49 us -> 2.88 us  [shards(): pl.pallas_call(sides, out_shape=tuple(state), in_specs=[in_vmem] * (4 + n...]
    ppermute x6, starting transfers between devices: 13.2 us -> 12.9 us  [swap(): return lax.ppermute(value, axis, pairs)]
    pallas_call x2 -> x3, Pallas kernels: 3.06 us -> 2.88 us  [do_middle(): pl.pallas_call(functools.partial(middle, jobs, h, p), out_shape=tuple(sta...]
  transfers between devices with their start and end apart: 6 -> 6, of which waited for: 0 -> 0; matrix products, arithmetic and copies ran while one was open for 0% -> 0% of each run, Pallas kernels for 28% -> 19%
where the time goes in v5:
time: 22.5 us; the launch traced here: 22.4 us
  starting transfers between devices  12.9 us (57%)
  Pallas kernels  8.79 us (39%)
  between operations  0.69 us (3%)
    ppermute x6, starting transfers between devices, swap(): return lax.ppermute(value, axis, pairs)  12.9 us
    pallas_call x3, Pallas kernels, do_middle(): pl.pallas_call(functools.partial(middle, jobs, h, p), out_shape=tuple(sta...  2.88 us
    pallas_call x1, Pallas kernels, shards(): pl.pallas_call(sides, out_shape=tuple(state), in_specs=[in_vmem] * (4 + n...  2.88 us
    pallas_call x1, Pallas kernels, shards(): pl.pallas_call(corners, out_shape=tuple(state) + (f32(16, 16, 128), f32(1...  1.79 us
    pallas_call x1, Pallas kernels, shards(): pl.pallas_call(pack_own, out_shape=(jax.ShapeDtypeStruct((16, 16, 128), j...  1.2 us
  transfers between devices with their start and end apart: 6, of which 0 were waited for; matrix products, arithmetic and copies ran while one was open for 0% of the time, Pallas kernels for 19%

profile of v5, /device:TPU:1, one launch (start us, length us, event | category | flops | bytes accessed | tf_op | source)
XLA Modules:
  0.0 22.4 jit_solution(12788897813695925279)
XLA Ops:
  0.6 1.2 %shard_map.58 = (s32[16,16,128]{2,1,0:T(8,128)S(1)}, f32[16,16,128]{2,1,0:T(8,128)S(1)}, f32[3,16,16,128]{3,2,1,0:T(8,128)S(1)}, f32[16,16,128]{2,1,0:T(8,128)S(...) custom-call(s32[16,16,128]{2,1,0:T(8,128)} %phase_in.1, ...), custom_call_target="tpu_custom_call" | custom-call | tf_op jit(solution)/shard_map/pallas_call | solution.py:563
  1.8 1.6 %shard_map.59 = (f32[24,40,128]{2,1,0:T(8,128)S(1)}, f32[4,24,40,128]{3,2,1,0:T(8,128)S(1)}, f32[19,22,32,128]{3,2,1,0:T(8,128)S(1)}, f32[19,22,32,128]{3,2,1,0:...) custom-call(s32[16,16,128]{2,1,0:T(8,128)S(1)} %get-tuple-element.59, ...), custom_call_target="tpu_custom_call", output_to_operand_aliasing={{10}: (3, {}), {11}: (4, {})} | custom-call | flops 40000000 | bytes 20000000 | tf_op jit(solution)/shard_map/pallas_call | solution.py:575
  3.5 2.0 %collective-permute-start = (f32[16,16,128]{2,1,0:T(8,128)S(1)}, f32[16,16,128]{2,1,0:T(8,128)S(1)}, u32[]{:S(2)}, u32[]{:S(2)}) collective-permute-start(f32[16,16,128]{2,1,0:T(8,128)S(1)} %get-tuple-element.64), channel_id=1, source_target_pairs={{0,1},{1,0},{2,3},{3,2},{4,5},{5,4},{6,7},{7,6},{8,9},{9,8},{10,11... | collective-permute-start | bytes 393224 | tf_op jit(solution)/shard_map/ppermute | solution.py:555
  5.5 1.2 %shard_map.60 = (f32[24,40,128]{2,1,0:T(8,128)S(1)}, f32[4,24,40,128]{3,2,1,0:T(8,128)S(1)}, f32[19,22,32,128]{3,2,1,0:T(8,128)S(1)}, f32[19,22,32,128]{3,2,1,0:...) custom-call(s32[16,16,128]{2,1,0:T(8,128)S(1)} %get-tuple-element.59, ...), custom_call_target="tpu_custom_call", output_to_operand_aliasing={{0}: (3, {}), {1}: (4, {}), {2}: (5, {}), {3}: (6, {}), {4}... | custom-call | flops 40000000 | bytes 20000000 | tf_op jit(solution)/shard_map/pallas_call | solution.py:575
  6.8 4.3 %collective-permute-start.1 = (f32[16,16,128]{2,1,0:T(8,128)S(1)}, f32[16,16,128]{2,1,0:T(8,128)S(1)}, u32[]{:S(2)}, u32[]{:S(2)}) collective-permute-start(f32[16,16,128]{2,1,0:T(8,128)S(1)} %get-tuple-element.76), channel_id=1, source_target_pairs={{1,2},{2,1},{3,4},{4,3},{5,6},{6,5},{7,8},{8,7},{9,10},{10,9},{11,... | collective-permute-start | bytes 393224 | tf_op jit(solution)/shard_map/ppermute | solution.py:555
  11.0 2.4 %collective-permute-start.4 = (f32[16,16,128]{2,1,0:T(8,128)S(1)}, f32[16,16,128]{2,1,0:T(8,128)S(1)}, u32[]{:S(2)}, u32[]{:S(2)}) collective-permute-start(f32[16,16,128]{2,1,0:T(8,128)S(1)} %get-tuple-element.90), channel_id=1, source_target_pairs={{16,32},{32,16},{48,64},{64,48},{80,96},{96,80},{112,128},{128,112... | collective-permute-start | bytes 393224 | tf_op jit(solution)/shard_map/ppermute | solution.py:555
  13.5 1.6 %collective-permute-start.5 = (f32[16,16,128]{2,1,0:T(8,128)S(1)}, f32[16,16,128]{2,1,0:T(8,128)S(1)}, u32[]{:S(2)}, u32[]{:S(2)}) collective-permute-start(f32[16,16,128]{2,1,0:T(8,128)S(1)} %get-tuple-element.91), channel_id=1, source_target_pairs={{0,16},{16,0},{32,48},{48,32},{64,80},{80,64},{96,112},{112,96},{1... | collective-permute-start | bytes 393224 | tf_op jit(solution)/shard_map/ppermute | solution.py:555
  15.1 0.0 collective-permute-done.from_ev.z_ev
  15.1 0.0 collective-permute-done.1.from_od.z_od
  15.1 0.1 shard_map.62
  15.2 2.5 %collective-permute-start.2 = (f32[16,8,128]{2,1,0:T(8,128)S(1)}, f32[16,8,128]{2,1,0:T(8,128)S(1)}, u32[]{:S(2)}, u32[]{:S(2)}) collective-permute-start(f32[16,8,128]{2,1,0:T(8,128)S(1)} %get-tuple-element.88), channel_id=1, source_target_pairs={{16,32},{32,16},{48,64},{64,48},{80,96},{96,80},{112,128},{128,112... | collective-permute-start | bytes 196616 | tf_op jit(solution)/shard_map/ppermute | solution.py:555
  17.7 0.0 collective-permute-start.3
  17.7 0.0 collective-permute-done.4.y_od
  17.7 0.0 collective-permute-done.5.y_ev
  17.7 2.9 %shard_map.63 = (f32[24,40,128]{2,1,0:T(8,128)S(1)}, f32[4,24,40,128]{3,2,1,0:T(8,128)S(1)}, f32[19,22,32,128]{3,2,1,0:T(8,128)S(1)}, f32[19,22,32,128]{3,2,1,0:...) custom-call(f32[16,16,128]{2,1,0:T(8,128)S(1)} %collective-permute-d, ...), custom_call_target="tpu_custom_call", output_to_operand_aliasing={{0}: (4, {}), {1}: (5, {}), {2}: (6, {}), {3}: (7, {}), {4}... | custom-call | flops 10000000 | bytes 5000000 | tf_op jit(solution)/shard_map/pallas_call | solution.py:601
  20.6 0.0 collective-permute-done.2.y_od
  20.6 0.0 collective-permute-done.3.y_ev
  20.6 1.8 %shard_map.64 = (f32[24,40,128]{2,1,0:T(8,128)S(1)}, f32[4,24,40,128]{3,2,1,0:T(8,128)S(1)}, f32[19,22,32,128]{3,2,1,0:T(8,128)S(1)}, f32[19,22,32,128]{3,2,1,0:...) custom-call(f32[16,8,128]{2,1,0:T(8,128)S(1)} %collective-permute-do, ...), custom_call_target="tpu_custom_call", output_to_operand_aliasing={{0}: (2, {}), {1}: (3, {}), {2}: (4, {}), {3}: (5, {}), {4}... | custom-call | tf_op jit(solution)/shard_map/pallas_call | solution.py:610
  (2 shorter events, 0.0 us)
Async XLA Ops:
  3.5 11.6 %collective-permute-start = (f32[16,16,128]{2,1,0:T(8,128)S(1)}, f32[16,16,128]{2,1,0:T(8,128)S(1)}, u32[]{:S(2)}, u32[]{:S(2)}) collective-permute-start(f32[16,16,128]{2,1,0:T(8,128)S(1)} %get-tuple-element.64), channel_id=1, source_target_pairs={{0,1},{1,0},{2,3},{3,2},{4,5},{5,4},{6,7},{7,6},{8,9},{9,8},{10,11... | collective-permute-start | bytes 393224 | tf_op jit(solution)/shard_map/ppermute | solution.py:555
  6.8 8.3 %collective-permute-start.1 = (f32[16,16,128]{2,1,0:T(8,128)S(1)}, f32[16,16,128]{2,1,0:T(8,128)S(1)}, u32[]{:S(2)}, u32[]{:S(2)}) collective-permute-start(f32[16,16,128]{2,1,0:T(8,128)S(1)} %get-tuple-element.76), channel_id=1, source_target_pairs={{1,2},{2,1},{3,4},{4,3},{5,6},{6,5},{7,8},{8,7},{9,10},{10,9},{11,... | collective-permute-start | bytes 393224 | tf_op jit(solution)/shard_map/ppermute | solution.py:555
  11.0 6.7 %collective-permute-start.4 = (f32[16,16,128]{2,1,0:T(8,128)S(1)}, f32[16,16,128]{2,1,0:T(8,128)S(1)}, u32[]{:S(2)}, u32[]{:S(2)}) collective-permute-start(f32[16,16,128]{2,1,0:T(8,128)S(1)} %get-tuple-element.90), channel_id=1, source_target_pairs={{16,32},{32,16},{48,64},{64,48},{80,96},{96,80},{112,128},{128,112... | collective-permute-start | bytes 393224 | tf_op jit(solution)/shard_map/ppermute | solution.py:555
  13.5 4.2 %collective-permute-start.5 = (f32[16,16,128]{2,1,0:T(8,128)S(1)}, f32[16,16,128]{2,1,0:T(8,128)S(1)}, u32[]{:S(2)}, u32[]{:S(2)}) collective-permute-start(f32[16,16,128]{2,1,0:T(8,128)S(1)} %get-tuple-element.91), channel_id=1, source_target_pairs={{0,16},{16,0},{32,48},{48,32},{64,80},{80,64},{96,112},{112,96},{1... | collective-permute-start | bytes 393224 | tf_op jit(solution)/shard_map/ppermute | solution.py:555
  15.2 5.4 %collective-permute-start.2 = (f32[16,8,128]{2,1,0:T(8,128)S(1)}, f32[16,8,128]{2,1,0:T(8,128)S(1)}, u32[]{:S(2)}, u32[]{:S(2)}) collective-permute-start(f32[16,8,128]{2,1,0:T(8,128)S(1)} %get-tuple-element.88), channel_id=1, source_target_pairs={{16,32},{32,16},{48,64},{64,48},{80,96},{96,80},{112,128},{128,112... | collective-permute-start | bytes 196616 | tf_op jit(solution)/shard_map/ppermute | solution.py:555
  17.7 2.9 %collective-permute-start.3 = (f32[16,8,128]{2,1,0:T(8,128)S(1)}, f32[16,8,128]{2,1,0:T(8,128)S(1)}, u32[]{:S(2)}, u32[]{:S(2)}) collective-permute-start(f32[16,8,128]{2,1,0:T(8,128)S(1)} %get-tuple-element.89), channel_id=1, source_target_pairs={{0,16},{16,0},{32,48},{48,32},{64,80},{80,64},{96,112},{112,96},{1... | collective-permute-start | bytes 196616 | tf_op jit(solution)/shard_map/ppermute | solution.py:555

commit v6 on v5

--- a/solution.py
+++ b/solution.py
@@ -443,7 +443,7 @@
                 lay(refs, at, y + 4, own_plane(at, y, phase, density, velocity))
             return carry
 
-        lax.fori_loop(0, 16, body, 0, unroll=2)
+        lax.fori_loop(0, 16, body, 0, unroll=4)
 
     parts = dict(
         l=lay_own,
@@ -486,7 +486,7 @@
                 frame_of(refs, at)[y + 4, 0:8, :] = fold_halo(at, low, high, y)
             return carry
 
-        lax.fori_loop(0, 16, body, 0, unroll=4)
+        lax.fori_loop(0, 16, body, 0, unroll=8)
 
     def assemble_y(odd):
         low, high = (y_ev, y_od) if odd else (y_od, y_ev)

time: 22.5 us -> 22.5 us (level)
  transfers between devices with their start and end apart: 6 -> 6, of which waited for: 0 -> 0; matrix products, arithmetic and copies ran while one was open for 0% -> 0% of each run, Pallas kernels for 19% -> 18%
where the time goes in v6:
time: 22.5 us; the launch traced here: 22.4 us
  starting transfers between devices  12.9 us (57%)
  Pallas kernels  8.75 us (39%)
  between operations  0.69 us (3%)
    ppermute x6, starting transfers between devices, swap(): return lax.ppermute(value, axis, pairs)  12.9 us
    pallas_call x3, Pallas kernels, do_middle(): pl.pallas_call(functools.partial(middle, jobs, h, p), out_shape=tuple(sta...  2.86 us
    pallas_call x1, Pallas kernels, shards(): pl.pallas_call(sides, out_shape=tuple(state), in_specs=[in_vmem] * (4 + n...  2.86 us
    pallas_call x1, Pallas kernels, shards(): pl.pallas_call(corners, out_shape=tuple(state) + (f32(16, 16, 128), f32(1...  1.79 us
    pallas_call x1, Pallas kernels, shards(): pl.pallas_call(pack_own, out_shape=(jax.ShapeDtypeStruct((16, 16, 128), j...  1.2 us
  transfers between devices with their start and end apart: 6, of which 0 were waited for; matrix products, arithmetic and copies ran while one was open for 0% of the time, Pallas kernels for 18%

profile of v6, /device:TPU:1, one launch (start us, length us, event | category | flops | bytes accessed | tf_op | source)
XLA Modules:
  0.0 22.4 jit_solution(2181756164843629871)
XLA Ops:
  0.6 1.2 %shard_map.58 = (s32[16,16,128]{2,1,0:T(8,128)S(1)}, f32[16,16,128]{2,1,0:T(8,128)S(1)}, f32[3,16,16,128]{3,2,1,0:T(8,128)S(1)}, f32[16,16,128]{2,1,0:T(8,128)S(...) custom-call(s32[16,16,128]{2,1,0:T(8,128)} %phase_in.1, ...), custom_call_target="tpu_custom_call" | custom-call | tf_op jit(solution)/shard_map/pallas_call | solution.py:563
  1.8 1.6 %shard_map.59 = (f32[24,40,128]{2,1,0:T(8,128)S(1)}, f32[4,24,40,128]{3,2,1,0:T(8,128)S(1)}, f32[19,22,32,128]{3,2,1,0:T(8,128)S(1)}, f32[19,22,32,128]{3,2,1,0:...) custom-call(s32[16,16,128]{2,1,0:T(8,128)S(1)} %get-tuple-element.59, ...), custom_call_target="tpu_custom_call", output_to_operand_aliasing={{10}: (3, {}), {11}: (4, {})} | custom-call | flops 40000000 | bytes 20000000 | tf_op jit(solution)/shard_map/pallas_call | solution.py:575
  3.5 2.1 %collective-permute-start = (f32[16,16,128]{2,1,0:T(8,128)S(1)}, f32[16,16,128]{2,1,0:T(8,128)S(1)}, u32[]{:S(2)}, u32[]{:S(2)}) collective-permute-start(f32[16,16,128]{2,1,0:T(8,128)S(1)} %get-tuple-element.64), channel_id=1, source_target_pairs={{0,1},{1,0},{2,3},{3,2},{4,5},{5,4},{6,7},{7,6},{8,9},{9,8},{10,11... | collective-permute-start | bytes 393224 | tf_op jit(solution)/shard_map/ppermute | solution.py:555
  5.5 1.2 %shard_map.60 = (f32[24,40,128]{2,1,0:T(8,128)S(1)}, f32[4,24,40,128]{3,2,1,0:T(8,128)S(1)}, f32[19,22,32,128]{3,2,1,0:T(8,128)S(1)}, f32[19,22,32,128]{3,2,1,0:...) custom-call(s32[16,16,128]{2,1,0:T(8,128)S(1)} %get-tuple-element.59, ...), custom_call_target="tpu_custom_call", output_to_operand_aliasing={{0}: (3, {}), {1}: (4, {}), {2}: (5, {}), {3}: (6, {}), {4}... | custom-call | flops 40000000 | bytes 20000000 | tf_op jit(solution)/shard_map/pallas_call | solution.py:575
  6.8 4.3 %collective-permute-start.1 = (f32[16,16,128]{2,1,0:T(8,128)S(1)}, f32[16,16,128]{2,1,0:T(8,128)S(1)}, u32[]{:S(2)}, u32[]{:S(2)}) collective-permute-start(f32[16,16,128]{2,1,0:T(8,128)S(1)} %get-tuple-element.76), channel_id=1, source_target_pairs={{1,2},{2,1},{3,4},{4,3},{5,6},{6,5},{7,8},{8,7},{9,10},{10,9},{11,... | collective-permute-start | bytes 393224 | tf_op jit(solution)/shard_map/ppermute | solution.py:555
  11.0 2.4 %collective-permute-start.4 = (f32[16,16,128]{2,1,0:T(8,128)S(1)}, f32[16,16,128]{2,1,0:T(8,128)S(1)}, u32[]{:S(2)}, u32[]{:S(2)}) collective-permute-start(f32[16,16,128]{2,1,0:T(8,128)S(1)} %get-tuple-element.90), channel_id=1, source_target_pairs={{16,32},{32,16},{48,64},{64,48},{80,96},{96,80},{112,128},{128,112... | collective-permute-start | bytes 393224 | tf_op jit(solution)/shard_map/ppermute | solution.py:555
  13.5 1.6 %collective-permute-start.5 = (f32[16,16,128]{2,1,0:T(8,128)S(1)}, f32[16,16,128]{2,1,0:T(8,128)S(1)}, u32[]{:S(2)}, u32[]{:S(2)}) collective-permute-start(f32[16,16,128]{2,1,0:T(8,128)S(1)} %get-tuple-element.91), channel_id=1, source_target_pairs={{0,16},{16,0},{32,48},{48,32},{64,80},{80,64},{96,112},{112,96},{1... | collective-permute-start | bytes 393224 | tf_op jit(solution)/shard_map/ppermute | solution.py:555
  15.1 0.0 collective-permute-done.from_ev.z_ev
  15.1 0.0 collective-permute-done.1.from_od.z_od
  15.1 0.1 shard_map.62
  15.2 2.5 %collective-permute-start.2 = (f32[16,8,128]{2,1,0:T(8,128)S(1)}, f32[16,8,128]{2,1,0:T(8,128)S(1)}, u32[]{:S(2)}, u32[]{:S(2)}) collective-permute-start(f32[16,8,128]{2,1,0:T(8,128)S(1)} %get-tuple-element.88), channel_id=1, source_target_pairs={{16,32},{32,16},{48,64},{64,48},{80,96},{96,80},{112,128},{128,112... | collective-permute-start | bytes 196616 | tf_op jit(solution)/shard_map/ppermute | solution.py:555
  17.7 0.0 collective-permute-start.3
  17.7 0.0 collective-permute-done.4.y_od
  17.7 0.0 collective-permute-done.5.y_ev
  17.7 2.9 %shard_map.63 = (f32[24,40,128]{2,1,0:T(8,128)S(1)}, f32[4,24,40,128]{3,2,1,0:T(8,128)S(1)}, f32[19,22,32,128]{3,2,1,0:T(8,128)S(1)}, f32[19,22,32,128]{3,2,1,0:...) custom-call(f32[16,16,128]{2,1,0:T(8,128)S(1)} %collective-permute-d, ...), custom_call_target="tpu_custom_call", output_to_operand_aliasing={{0}: (4, {}), {1}: (5, {}), {2}: (6, {}), {3}: (7, {}), {4}... | custom-call | flops 10000000 | bytes 5000000 | tf_op jit(solution)/shard_map/pallas_call | solution.py:601
  20.6 0.0 collective-permute-done.2.y_od
  20.6 0.0 collective-permute-done.3.y_ev
  20.6 1.8 %shard_map.64 = (f32[24,40,128]{2,1,0:T(8,128)S(1)}, f32[4,24,40,128]{3,2,1,0:T(8,128)S(1)}, f32[19,22,32,128]{3,2,1,0:T(8,128)S(1)}, f32[19,22,32,128]{3,2,1,0:...) custom-call(f32[16,8,128]{2,1,0:T(8,128)S(1)} %collective-permute-do, ...), custom_call_target="tpu_custom_call", output_to_operand_aliasing={{0}: (2, {}), {1}: (3, {}), {2}: (4, {}), {3}: (5, {}), {4}... | custom-call | tf_op jit(solution)/shard_map/pallas_call | solution.py:610
  (2 shorter events, 0.0 us)
Async XLA Ops:
  3.5 11.6 %collective-permute-start = (f32[16,16,128]{2,1,0:T(8,128)S(1)}, f32[16,16,128]{2,1,0:T(8,128)S(1)}, u32[]{:S(2)}, u32[]{:S(2)}) collective-permute-start(f32[16,16,128]{2,1,0:T(8,128)S(1)} %get-tuple-element.64), channel_id=1, source_target_pairs={{0,1},{1,0},{2,3},{3,2},{4,5},{5,4},{6,7},{7,6},{8,9},{9,8},{10,11... | collective-permute-start | bytes 393224 | tf_op jit(solution)/shard_map/ppermute | solution.py:555
  6.8 8.3 %collective-permute-start.1 = (f32[16,16,128]{2,1,0:T(8,128)S(1)}, f32[16,16,128]{2,1,0:T(8,128)S(1)}, u32[]{:S(2)}, u32[]{:S(2)}) collective-permute-start(f32[16,16,128]{2,1,0:T(8,128)S(1)} %get-tuple-element.76), channel_id=1, source_target_pairs={{1,2},{2,1},{3,4},{4,3},{5,6},{6,5},{7,8},{8,7},{9,10},{10,9},{11,... | collective-permute-start | bytes 393224 | tf_op jit(solution)/shard_map/ppermute | solution.py:555
  11.0 6.7 %collective-permute-start.4 = (f32[16,16,128]{2,1,0:T(8,128)S(1)}, f32[16,16,128]{2,1,0:T(8,128)S(1)}, u32[]{:S(2)}, u32[]{:S(2)}) collective-permute-start(f32[16,16,128]{2,1,0:T(8,128)S(1)} %get-tuple-element.90), channel_id=1, source_target_pairs={{16,32},{32,16},{48,64},{64,48},{80,96},{96,80},{112,128},{128,112... | collective-permute-start | bytes 393224 | tf_op jit(solution)/shard_map/ppermute | solution.py:555
  13.5 4.2 %collective-permute-start.5 = (f32[16,16,128]{2,1,0:T(8,128)S(1)}, f32[16,16,128]{2,1,0:T(8,128)S(1)}, u32[]{:S(2)}, u32[]{:S(2)}) collective-permute-start(f32[16,16,128]{2,1,0:T(8,128)S(1)} %get-tuple-element.91), channel_id=1, source_target_pairs={{0,16},{16,0},{32,48},{48,32},{64,80},{80,64},{96,112},{112,96},{1... | collective-permute-start | bytes 393224 | tf_op jit(solution)/shard_map/ppermute | solution.py:555
  15.2 5.4 %collective-permute-start.2 = (f32[16,8,128]{2,1,0:T(8,128)S(1)}, f32[16,8,128]{2,1,0:T(8,128)S(1)}, u32[]{:S(2)}, u32[]{:S(2)}) collective-permute-start(f32[16,8,128]{2,1,0:T(8,128)S(1)} %get-tuple-element.88), channel_id=1, source_target_pairs={{16,32},{32,16},{48,64},{64,48},{80,96},{96,80},{112,128},{128,112... | collective-permute-start | bytes 196616 | tf_op jit(solution)/shard_map/ppermute | solution.py:555
  17.7 2.9 %collective-permute-start.3 = (f32[16,8,128]{2,1,0:T(8,128)S(1)}, f32[16,8,128]{2,1,0:T(8,128)S(1)}, u32[]{:S(2)}, u32[]{:S(2)}) collective-permute-start(f32[16,8,128]{2,1,0:T(8,128)S(1)} %get-tuple-element.89), channel_id=1, source_target_pairs={{0,16},{16,0},{32,48},{48,32},{64,80},{80,64},{96,112},{112,96},{1... | collective-permute-start | bytes 196616 | tf_op jit(solution)/shard_map/ppermute | solution.py:555
